TPU v7x, 512 devices: a whole 4x4x16 slice. The times are simulated.
512 devices in a mesh: sample: 4 (over x), variant: 16 (over z_lo, y), protein: 8 (over z_hi, core).
Axes of the slice: x: 4, y: 4, z: 16 (z_hi: 4, z_lo: 4; z = z_hi * 4 + z_lo), core: 2. Of those that a mesh axis runs over, the one named last changes fastest.
Arguments:
- dosages: bfloat16 [4096, 16384], P('sample', 'variant'), may hold values from 0 to 2
- proteins: bfloat16 [4096, 2048], P('sample', 'protein'), may hold values from -6 to 6
- covariates: float32 [44, 4096], P(None, 'sample'), may hold values from 0 to 2
- hit_index: int32 [64, 32, 128], P(None, 'protein'), may hold values from 0 to 16383, as said below
- hit_count: int32 [64, 32], P(None, 'protein'), may hold values from 1 to 128, as said below
Outputs:
- zscores: float32 [16384, 2048], P('variant', 'protein')
- hit_gram: float32 [2048, 128, 128], P(('sample', 'variant', 'protein'))
Inputs may be any that keep to these rules, and one draw needn't show every extreme that they name: `hit_count`: entry [g, i] is protein g * 32 + i. In every aligned block of 4 proteins the counts sum to exactly 256, and one of them is 128. `hit_index`: entry [g, i, j] is slot j of protein g * 32 + i. For j below the protein's count it is a slab variant, all distinct within one protein; other slots hold 0. Variant block b holds the variants b * 1024 to (b + 1) * 1024 - 1. In every aligned block of 4 proteins exactly 48 live hits lie in one variant block, and the other live hits are spread over the other blocks as evenly as possible.
All inputs are finite; a program needn't handle non-finite values.
Results may differ from a plain program's by a relative error of at most 0.025.
Values may be sent and summed in bfloat16 or wider, within the bound.
A program may use at most 64 MiB of HBM per device.

v0:
```python
import jax
import jax.numpy as jnp
from jax import lax
from jax.sharding import PartitionSpec as P

AVG_HITS = 16


def shards(dosages, proteins, covariates, hit_index, hit_count):
    largest_value = lax.Precision.HIGHEST
    n_sample = lax.axis_size("sample")
    n_variant = lax.axis_size("variant")
    rows_dev, v_dev = dosages.shape
    n_cov = covariates.shape[0]
    samples = rows_dev * n_sample
    n_dest, p_own, hit_slots = hit_index.shape
    block_hits = max(p_own * AVG_HITS, 2 * hit_slots)
    capacity = 3 * block_hits // n_variant
    my_block = lax.axis_index("variant")
    my_group = lax.axis_index("sample") * n_variant + my_block
    gram_part = jnp.dot(covariates, covariates.T, precision=largest_value)
    prot_part = jnp.dot(
        covariates, proteins, precision=largest_value, preferred_element_type=jnp.float32
    )
    dos_part = jnp.dot(
        covariates, dosages, precision=largest_value, preferred_element_type=jnp.float32
    )
    sq_part = jnp.sum(jnp.square(dosages.astype(jnp.float32)), axis=0)
    gram_cov, cov_prot, cov_dos, dos_sq = lax.psum(
        (gram_part, prot_part, dos_part, sq_part), "sample"
    )
    factor = jnp.linalg.cholesky(gram_cov)
    identity = jnp.eye(n_cov, dtype=jnp.float32)
    inverse_factor = jax.scipy.linalg.solve_triangular(factor, identity, lower=True)
    coef_mat = jnp.dot(
        inverse_factor.T,
        jnp.dot(inverse_factor, cov_prot, precision=largest_value),
        precision=largest_value,
    )
    fitted = jnp.einsum("cs,cp->sp", covariates, coef_mat, precision=largest_value)
    residual = (proteins.astype(jnp.float32) - fitted).astype(jnp.bfloat16)
    residual_squares_slab = jnp.sum(jnp.square(residual.astype(jnp.float32)), axis=0)
    whiten = jnp.dot(inverse_factor, cov_dos, precision=largest_value)
    dos_var = dos_sq - jnp.sum(whiten * whiten, axis=0)
    freedom = jnp.float32(samples - n_cov)
    index_all = hit_index.reshape(n_dest, p_own * hit_slots)
    slot_ids = jnp.arange(hit_slots, dtype=jnp.int32)
    live_all = (slot_ids[None, None, :] < hit_count[:, :, None]).reshape(n_dest, -1)
    selected = live_all & (index_all // v_dev == my_block)
    rank_all = jnp.cumsum(selected.astype(jnp.int32), axis=1) - 1
    slot_of = jnp.where(selected, rank_all, capacity)
    slab_column = index_all - my_block * v_dev
    dest_ids = jnp.arange(n_dest, dtype=jnp.int32)[:, None]
    col_index = (
        jnp.zeros((n_dest, capacity), jnp.int32).at[dest_ids, slot_of].set(slab_column, mode="drop")
    )
    outgoing = jnp.take(dosages, col_index.reshape(-1), axis=1)
    score_part = lax.dot_general(
        dosages, residual, (((0,), (0,)), ((), ())), preferred_element_type=jnp.float32
    )
    received = lax.all_to_all(
        outgoing, ("sample", "variant"), split_axis=1, concat_axis=1, tiled=True
    )
    own_index = lax.dynamic_index_in_dim(hit_index, my_group, 0, keepdims=False)
    own_count = lax.dynamic_index_in_dim(hit_count, my_group, 0, keepdims=False)
    live_slot = (slot_ids[None, :] < own_count[:, None]).reshape(-1)
    block_of = (own_index // v_dev).reshape(-1)
    onehot = (
        (block_of[:, None] == jnp.arange(n_variant, dtype=jnp.int32)[None, :]) & live_slot[:, None]
    ).astype(jnp.int32)
    before = jnp.cumsum(onehot, axis=0) - onehot
    rank_in = jnp.sum(before * onehot, axis=1)
    sources = jnp.arange(n_sample, dtype=jnp.int32)[:, None] * n_variant
    positions = (sources + block_of[None, :]) * capacity + rank_in[None, :]
    positions = jnp.where(live_slot[None, :], positions, 0)
    flat_count = p_own * hit_slots
    hit_cols = jnp.take(received, positions.reshape(-1), axis=1).reshape(
        rows_dev, n_sample, flat_count
    )
    hit_cols = jnp.where(live_slot[None, None, :], hit_cols, jnp.zeros((), jnp.bfloat16))
    hit_grid = hit_cols.reshape(rows_dev, n_sample, p_own, hit_slots)
    hit_prod = jnp.einsum("rqpa,rqpb->pab", hit_grid, hit_grid, preferred_element_type=jnp.float32)
    cov_all = lax.all_gather(covariates, "sample", axis=1, tiled=True)
    cov_grid = cov_all.reshape(n_cov, n_sample, rows_dev)
    hit_covariate_matrix = jnp.einsum(
        "cqr,rqk->ck",
        cov_grid,
        hit_cols,
        precision=largest_value,
        preferred_element_type=jnp.float32,
    )
    decorrelated_scores = jnp.dot(
        inverse_factor, hit_covariate_matrix, precision=largest_value
    ).reshape(n_cov, p_own, hit_slots)
    adjustment_term = jnp.einsum(
        "zwr,zwj->wrj", decorrelated_scores, decorrelated_scores, precision=largest_value
    )
    hit_gram = (hit_prod - adjustment_term) / jnp.float32(samples)
    score_sum, rss_total = lax.psum((score_part, residual_squares_slab), "sample")
    zscores = score_sum / jnp.sqrt(dos_var[:, None] * (rss_total[None, :] / freedom + 1e-05))
    return (zscores, hit_gram)


def solution(mesh):
    in_specs = (
        P("sample", "variant"),
        P("sample", "protein"),
        P(None, "sample"),
        P(None, "protein", None),
        P(None, "protein"),
    )
    out_specs = (P("variant", "protein"), P(("sample", "variant", "protein"), None, None))
    return jax.shard_map(shards, mesh=mesh, in_specs=in_specs, out_specs=out_specs, check_vma=False)
```

profile of v0, /device:TPU:1, one launch (start us, length us, event | category | flops | bytes accessed | tf_op | source)
XLA Modules:
  0.0 369.9 jit_solution(16705104994718637438)
XLA Ops:
  7.2 0.8 copy.43
  8.0 1.0 reshape.481
  8.9 1.0 fusion.31
  9.9 1.2 reduce-window.16
  12.0 0.8 multiply_reduce_fusion.2
  12.8 0.8 and_reduce_fusion
  13.6 0.9 broadcast_subtract_fusion
  14.5 120.1 %scatter_custom_fusion = s32[3072]{0:T(1024)S(1)} fusion(s32[32768]{0:T(1024)S(1)} %bitcast.127, s32[32768]{0:T(1024)S(1)} %bitcast.128, s32[]{:T(128)} %constant.136.clone.1), kind=kCustom, calls=%fused_computation.91 | custom fusion | bytes 12292
  135.0 2.9 copy.32
  137.9 14.0 %gather_fusion = bf16[3072,1024]{1,0:T(8,128)(2,1)} fusion(bf16[1024,1024]{0,1:T(8,128)(2,1)S(1)} %copy.32, s32[3072]{0:T(1024)S(1)} %broadcast_clamp_fusion), kind=kCustom, calls=%fused_computation | custom fusion | bytes 12595200 | tf_op jit(solution)/shard_map/jit(_take)/gather | solution.py:57
  151.9 6.6 %broadcast_select_fusion = bf16[1024,64,48]{0,2,1:T(8,128)(2,1)} fusion(bf16[1024,64,48]{0,2,1:T(8,128)(2,1)} %bitcast.122, pred[64,48]{1,0:T(8,128)(4,1)S(1)} %copy.30), kind=kLoop, calls=%fused_computation.3 | loop fusion | flops 3145728 | bytes 12585984 | tf_op jit(solution)/shard_map/jit(_take)/select_n | solution.py:57
  158.6 12.9 %all-to-all-start = ((bf16[1024,64,48]{0,2,1:T(8,128)(2,1)}), bf16[1024,64,48]{0,2,1:T(8,128)(2,1)}, u32[]{:S(2)}, u32[]{:S(2)}) async-start(bf16[1024,64,48]{0,2,1:T(8,128)(2,1)} %broadcast_select_fusion), calls=%async_computation | async-start | bytes 12582912 | tf_op jit(solution)/shard_map/all_to_all | solution.py:61
  172.5 48.3 %all-reduce.1 = (f32[44,44]{0,1:T(8,128)S(1)}, f32[44,256]{1,0:T(8,128)S(1)}) all-reduce(f32[44,44]{0,1:T(8,128)S(1)} %fusion.57, f32[44,256]{1,0:T(8,128)S(1)} %fusion.58), channel_id=1, replica_groups=mesh['sample'=4,'variant'=16,'protein'=8] {'sample'}, use_global_device_ids=true, to_apply=%region_0.0 | all-reduce | flops 13200 | bytes 105600 | tf_op jit(solution)/shard_map/psum | solution.py:29
  220.9 4.0 %cholesky.17 = f32[44,44]{1,0:T(8,128)S(1)} custom-call(f32[44,44]{1,0:T(8,128)S(1)} %fusion.43), custom_call_target="Cholesky" | custom-call | tf_op jit(solution)/shard_map/jit(cholesky)/cholesky | solution.py:32
  225.6 0.7 fusion.40
  226.2 3.4 custom-call.7
  230.3 1.2 multiply_reduce_fusion.1
  231.4 1.9 fusion.61
  233.3 1.7 convolution_bitcast_fusion
  235.2 0.7 add_select_fusion.4
  236.0 1.2 reduce-window.14
  237.9 7.0 %all-reduce = (f32[256]{0:T(256)S(1)}, f32[1024]{0:T(1024)S(1)}) all-reduce(f32[256]{0:T(256)S(1)} %get-tuple-element.12, f32[1024]{0:T(1024)S(1)} %multiply_reduce_fusion), channel_id=1, replica_groups=mesh['sample'=4,'variant'=16,'protein'=8] {'sample'}, use_global_device_ids=true, to_apply=%region_10.11 | all-reduce | flops 1280 | bytes 10240 | tf_op jit(solution)/shard_map/psum | solution.py:99
  244.9 0.7 add_select_fusion.3
  245.8 12.8 %all_gather.3 = f32[44,4096]{1,0:T(8,128)S(1)} all-gather(f32[44,1024]{1,0:T(8,128)S(1)} %copy-done.1), channel_id=1, replica_groups=mesh['sample'=4,'variant'=16,'protein'=8] {'sample'}, dimensions={1}, use_global_device_ids=true | all-gather | bytes 901120 | tf_op jit(solution)/shard_map/all_gather | solution.py:83
  259.3 72.6 %all-reduce.5.cloned.1.call-done = (f32[1024,256]{0,1:T(8,128)}, f32[44,1024]{1,0:T(8,128)}) async-done(((f32[1024,256]{0,1:T(8,128)}, f32[44,1024]{1,0:T(8,128)}), (f32[1024,256]{0,1:T(8,128)}, f32[44,1024]{1,0:T(8,128)})) %all-reduce.5.cloned.1.call-update) | async-done | bytes 1228816 | tf_op jit(solution)/shard_map/psum | solution.py:99
  331.9 1.2 fusion.23
  333.2 1.4 rsqrt_multiply_fusion
  334.6 1.3 copy.37
  335.9 14.6 %gather_fusion.1 = bf16[2048,1024]{1,0:T(8,128)(2,1)} fusion(bf16[1024,3072]{0,1:T(8,128)(2,1)} %bitcast.16, s32[2048]{0:T(1024)S(1)} %broadcast_clamp_fusion.1), kind=kCustom, calls=%fused_computation.1 | custom fusion | bytes 8396800 | tf_op jit(solution)/shard_map/jit(_take)/gather | solution.py:77
  350.6 6.1 %fusion.16 = f32[512,44]{1,0:T(8,128)S(1)} fusion(bf16[1024,4,512]{0,2,1:T(8,128)(2,1)} %bitcast.123, pred[512]{0:T(512)(128)(4,1)S(1)} %bitcast_compare_fusion, pred[4,512]{1,0:T(4,128)(4,1)S(1)} %compare_and_fusion.1, f32[44,4,1024]{2,1,0:T(4,128)S(1)} %reshape.484), kind=kOutput, calls=%fused_computation.24 | convolution fusion | flops 1111490560 | bytes 5007872 | tf_op jit(solution)/shard_map/cqr,rqk->ck/dot_general | solution.py:85
  357.0 4.7 %fusion.20 = f32[4,128,128]{2,1,0:T(8,128)S(1)} fusion(bf16[1024,4,4,128]{0,3,2,1:T(8,128)(2,1)} %bitcast.124, pred[4,4,128]{2,0,1:T(4,128)(4,1)S(1)} %compare_and_fusion.2, pred[4,128]{1,0:T(4,128)(4,1)S(1)} %iota_compare_fusion.6), kind=kOutput, calls=%fused_computation.27 | convolution fusion | flops 541065216 | bytes 4459008 | tf_op jit(solution)/shard_map/rqpa,rqpb->pab/dot_general | solution.py:82
  361.7 1.3 fusion.19
  (62 shorter events, 6.0 us)
Async XLA Ops:
  158.6 13.0 %copy-start.2 = (bf16[1024,256]{1,0:T(8,128)(2,1)S(1)}, bf16[1024,256]{1,0:T(8,128)(2,1)}, u32[]{:S(2)}) copy-start(bf16[1024,256]{1,0:T(8,128)(2,1)} %param.6) | copy-start | bytes 1572868
  158.6 13.2 %copy-start.1 = (f32[44,1024]{1,0:T(8,128)S(1)}, f32[44,1024]{1,0:T(8,128)}, u32[]{:S(2)}) copy-start(f32[44,1024]{1,0:T(8,128)} %param.7) | copy-start | bytes 540676
  158.6 177.4 %all-to-all-start = ((bf16[1024,64,48]{0,2,1:T(8,128)(2,1)}), bf16[1024,64,48]{0,2,1:T(8,128)(2,1)}, u32[]{:S(2)}, u32[]{:S(2)}) async-start(bf16[1024,64,48]{0,2,1:T(8,128)(2,1)} %broadcast_select_fusion), calls=%async_computation | async-start | bytes 12582912 | tf_op jit(solution)/shard_map/all_to_all | solution.py:61
  171.5 59.9 %copy-start = (bf16[1024,1024]{1,0:T(8,128)(2,1)S(1)}, bf16[1024,1024]{1,0:T(8,128)(2,1)}, u32[]{:S(2)}) copy-start(bf16[1024,1024]{1,0:T(8,128)(2,1)} %param.5) | copy-start | bytes 6291460
  171.5 160.4 %all-reduce.5.cloned.1.call-start = ((), (), s32[]{:S(2)}) async-start(), calls=%async_computation.1 | async-start | bytes 2490368 | tf_op jit(solution)/shard_map/psum | solution.py:99
  230.3 4.8 %copy-start.3 = (s32[64,4]{0,1:T(4,128)S(1)}, s32[64,4]{0,1:T(4,128)}, u32[]{:S(2)}) copy-start(s32[64,4]{0,1:T(4,128)} %param.9) | copy-start | bytes 3076
Sparse Core Ops, SparseCore 0:
  235.1 96.7 all-reduce.4
where the time goes:
time: 371 us; the launch traced here: 370 us
  local copies, waits for them, and re-layouts  157 us (42%)
  waiting for transfers between devices  72.6 us (20%)
  blocking collectives  68.1 us (18%)
  other arithmetic  25.3 us (7%)
  matrix products  19.6 us (5%)
  between operations  14.4 us (4%)
  starting transfers between devices  13 us (4%)
    unnamed x16, local copies, waits for them, and re-layouts  125 us
    psum x1, waiting for transfers between devices, shards(): lax.psum((score_part, residual_squares_slab), 'sample')  72.6 us
    psum x1, blocking collectives, shards(): lax.psum((gram_part, prot_part, dos_part, sq_part), 'sample')  48.3 us
    gather x1, local copies, waits for them, and re-layouts, shards(): jnp.take(received, positions.reshape(-1), axis=1)  14.6 us
    gather x1, local copies, waits for them, and re-layouts, shards(): outgoing = jnp.take(dosages, col_index.reshape(-1), axis=1)  14 us
    all_to_all x1, starting transfers between devices, shards(): lax.all_to_all(outgoing, ('sample', 'variant'), split_axis=1, concat_axis...  12.9 us
    all_gather x1, blocking collectives, shards(): cov_all = lax.all_gather(covariates, 'sample', axis=1, tiled=True)  12.8 us
  transfers between devices with their start and end apart: 2, of which 1 were waited for; matrix products, arithmetic and copies ran while one was open for 6% of the time, Pallas kernels for 0%

commit v1 on v0

v1 whole, which is shorter than its diff:
```python
import jax
import jax.numpy as jnp
from jax import lax
from jax.sharding import PartitionSpec as P

BF16 = jnp.bfloat16
F32 = jnp.float32


def shards(dosages, proteins, covariates, hit_index, hit_count):
    best = lax.Precision.HIGHEST
    n_sample = lax.axis_size("sample")
    n_variant = lax.axis_size("variant")
    rows, v_dev = dosages.shape
    n_prot = proteins.shape[1]
    n_cov = covariates.shape[0]
    samples = rows * n_sample
    n_dest, p_own, slots = hit_index.shape
    flat = p_own * slots
    capacity = 3 * max(p_own * 16, 2 * slots) // n_variant
    my_block = lax.axis_index("variant")

    dos_part = jnp.dot(covariates, dosages, precision=best, preferred_element_type=F32)
    prot_part = jnp.dot(covariates, proteins, precision=best, preferred_element_type=F32)
    gram_part = jnp.dot(covariates, covariates.T, precision=best)
    total = lax.psum(jnp.concatenate([dos_part, prot_part, gram_part], axis=1), "sample")
    gram_cov = total[:, v_dev + n_prot :]
    factor = jnp.linalg.cholesky(gram_cov)
    inverse_factor = jax.scipy.linalg.solve_triangular(
        factor, jnp.eye(n_cov, dtype=F32), lower=True
    )
    coef = jnp.dot(
        inverse_factor.T,
        jnp.dot(inverse_factor, total[:, : v_dev + n_prot], precision=best),
        precision=best,
    )
    fitted = jnp.einsum("cs,cp->sp", covariates, coef, precision=best)
    dos_res = (dosages.astype(F32) - fitted[:, :v_dev]).astype(BF16)
    prot_res = (proteins.astype(F32) - fitted[:, v_dev:]).astype(BF16)

    index_all = hit_index.reshape(n_dest, flat)
    slot_ids = jnp.arange(slots, dtype=jnp.int32)
    live_all = (slot_ids[None, None, :] < hit_count[:, :, None]).reshape(n_dest, flat)
    upper = jnp.triu(jnp.ones((flat, flat), BF16))
    chosen = live_all & (index_all // v_dev == my_block)
    rank = jnp.dot(chosen.astype(BF16), upper, preferred_element_type=F32).astype(jnp.int32) - 1
    rank = jnp.where(chosen, rank, -1)
    local = index_all - my_block * v_dev + 1
    places = jnp.arange(capacity, dtype=jnp.int32)
    col_index = jnp.sum(
        jnp.where(rank[:, None, :] == places[None, :, None], local[:, None, :], 0), axis=2
    )
    pick = (
        col_index.reshape(-1)[:, None] == jnp.arange(1, v_dev + 1, dtype=jnp.int32)[None, :]
    ).astype(BF16)
    outgoing = lax.dot_general(
        pick, dos_res, (((1,), (1,)), ((), ())), preferred_element_type=F32
    ).astype(BF16)
    received = lax.all_to_all(
        outgoing.reshape(n_sample, n_variant, capacity, rows),
        "variant",
        split_axis=1,
        concat_axis=1,
        tiled=True,
    ).reshape(n_sample, n_variant * capacity, rows)

    score = lax.dot_general(
        dos_res, prot_res, (((0,), (0,)), ((), ())), preferred_element_type=F32
    ).astype(BF16)
    squares = jnp.concatenate(
        [
            jnp.sum(jnp.square(dos_res.astype(F32)), axis=0),
            jnp.sum(jnp.square(prot_res.astype(F32)), axis=0),
        ]
    )
    squares = lax.psum(squares, "sample")
    own = v_dev // n_sample
    score = lax.psum_scatter(score, "sample", scatter_dimension=0, tiled=True).astype(F32)
    dos_var = lax.dynamic_slice(squares, (lax.axis_index("sample") * own,), (own,))
    rss = squares[v_dev:]
    z = score / jnp.sqrt(dos_var[:, None] * (rss[None, :] / F32(samples - n_cov) + 1e-05))
    zscores = lax.all_gather(z.astype(BF16), "sample", axis=0, tiled=True).astype(F32)

    own_index = lax.dynamic_slice_in_dim(
        index_all.reshape(n_sample, n_variant, flat), my_block, 1, axis=1
    )[:, 0]
    own_live = lax.dynamic_slice_in_dim(
        live_all.reshape(n_sample, n_variant, flat), my_block, 1, axis=1
    )[:, 0]
    block_of = own_index // v_dev
    member = (
        block_of[:, None, :] == jnp.arange(n_variant, dtype=jnp.int32)[None, :, None]
    ) & own_live[:, None, :]
    upto = jnp.dot(
        member.astype(BF16).reshape(-1, flat), upper, preferred_element_type=F32
    ).reshape(member.shape)
    rank_in = jnp.sum(jnp.where(member, upto, 0.0), axis=1).astype(jnp.int32) - 1
    position = jnp.where(own_live, block_of * capacity + rank_in, -1)
    place = (
        position[:, :, None] == jnp.arange(n_variant * capacity, dtype=jnp.int32)[None, None, :]
    ).astype(BF16)
    cols = (
        jnp.einsum("sjk,skr->sjr", place, received, preferred_element_type=F32)
        .astype(BF16)
        .reshape(n_sample, p_own, slots, rows)
    )
    gram = jnp.einsum("spar,spbr->spab", cols, cols, preferred_element_type=F32)
    gram = lax.psum_scatter(gram.astype(BF16), "sample", scatter_dimension=0, tiled=False)
    return (zscores, gram.astype(F32) / F32(samples))


def solution(mesh):
    in_specs = (
        P("sample", "variant"),
        P("sample", "protein"),
        P(None, "sample"),
        P(None, "protein", None),
        P(None, "protein"),
    )
    out_specs = (P("variant", "protein"), P(("sample", "variant", "protein"), None, None))
    return jax.shard_map(shards, mesh=mesh, in_specs=in_specs, out_specs=out_specs, check_vma=False)
```

time: 371 us -> 297 us (0.80)
  local copies, waits for them, and re-layouts: 157 us -> 11.5 us
  waiting for transfers between devices: 72.6 us -> 199 us
  blocking collectives: 68.1 us -> 19.2 us
  other arithmetic: 25.3 us -> 16.8 us
  matrix products: 19.6 us -> 27.9 us
  starting transfers between devices: 13 us -> 7.38 us
    unnamed x16 -> x14, local copies, waits for them, and re-layouts: 125 us -> 2.35 us
    all_to_all x1, waiting for transfers between devices: 0.01 us -> 111 us  [shards(): lax.all_to_all(outgoing.reshape(n_sample, n_variant, capacity, rows), 'va...]
    psum x2 -> x1, blocking collectives: 55.3 us -> 8.39 us  [shards(): squares = lax.psum(squares, 'sample')]
    gather x2 -> x0, local copies, waits for them, and re-layouts: 28.6 us -> none  [the longest x1 14.6 us: shards(): jnp.take(received, positions.reshape(-1), axis=1)]
    reduce_scatter x0 -> x2, waiting for transfers between devices: none -> 26.7 us  [the longest x1 26.6 us: shards(): lax.psum_scatter(gram.astype(BF16), 'sample', scatter_dimension=0, tiled=...]
    psum x1, waiting for transfers between devices: 72.6 us -> 60.6 us  [shards(): lax.psum(jnp.concatenate([dos_part, prot_part, gram_part], axis=1), 'samp...]
    dot_general x12, matrix products: 19.4 us -> 27.7 us  [the longest x1 7.15 us: shards(): lax.dot_general(pick, dos_res, (((1,), (1,)), ((), ())), preferred_elemen...]
    select_n x6 -> x1, other arithmetic: 8.17 us -> 0.02 us  [shards(): position = jnp.where(own_live, block_of * capacity + rank_in, -1)]
  transfers between devices with their start and end apart: 2 -> 4, of which waited for: 1 -> 3; matrix products, arithmetic and copies ran while one was open for 6% -> 6% of each run, Pallas kernels for 0% -> 0%
where the time goes in v1:
time: 297 us; the launch traced here: 295 us
  waiting for transfers between devices  199 us (67%)
  matrix products  27.9 us (9%)
  blocking collectives  19.2 us (6%)
  other arithmetic  16.8 us (6%)
  between operations  14.1 us (5%)
  local copies, waits for them, and re-layouts  11.5 us (4%)
  starting transfers between devices  7.38 us (2%)
    all_to_all x1, waiting for transfers between devices, shards(): lax.all_to_all(outgoing.reshape(n_sample, n_variant, capacity, rows), 'va...  111 us
    psum x1, waiting for transfers between devices, shards(): lax.psum(jnp.concatenate([dos_part, prot_part, gram_part], axis=1), 'samp...  60.6 us
    reduce_scatter x1, waiting for transfers between devices, shards(): lax.psum_scatter(gram.astype(BF16), 'sample', scatter_dimension=0, tiled=...  26.6 us
    all_gather x1, blocking collectives, shards(): lax.all_gather(z.astype(BF16), 'sample', axis=0, tiled=True).astype(F32)  10.8 us
    psum x1, blocking collectives, shards(): squares = lax.psum(squares, 'sample')  8.39 us
    all_to_all x1, starting transfers between devices, shards(): lax.all_to_all(outgoing.reshape(n_sample, n_variant, capacity, rows), 'va...  7.25 us
    dot_general x1, matrix products, shards(): lax.dot_general(pick, dos_res, (((1,), (1,)), ((), ())), preferred_elemen...  7.15 us
  transfers between devices with their start and end apart: 4, of which 3 were waited for; matrix products, arithmetic and copies ran while one was open for 6% of the time, Pallas kernels for 0%

profile of v1, /device:TPU:1, one launch (start us, length us, event | category | flops | bytes accessed | tf_op | source)
XLA Modules:
  0.0 295.3 jit_solution(17184688388187104375)
XLA Ops:
  7.2 0.9 copy-done
  8.4 1.4 fusion.75
  9.8 2.8 fusion.74
  12.6 1.1 copy.30
  14.4 1.2 select_reduce_fusion
  15.6 60.6 %all-reduce.2.cloned.1.call-done = f32[44,1324]{0,1:T(8,128)} async-done(((f32[44,1324]{0,1:T(8,128)}), f32[44,1324]{0,1:T(8,128)}) %all-reduce.2.cloned.1.call-update) | async-done | bytes 233040 | tf_op jit(solution)/shard_map/psum | solution.py:26
  76.2 0.7 slice.32
  77.1 0.7 fusion.51
  77.8 4.0 %cholesky.17 = f32[44,44]{1,0:T(8,128)S(1)} custom-call(f32[44,44]{1,0:T(8,128)S(1)} %fusion.51), custom_call_target="Cholesky" | custom-call | tf_op jit(solution)/shard_map/jit(cholesky)/cholesky | solution.py:28
  81.9 0.6 compare_reduce_fusion
  82.5 0.7 fusion.48
  83.2 3.4 %custom-call.7 = f32[1,44,44]{1,2,0:T(8,128)S(1)} custom-call(f32[1,44,44]{2,1,0:T(8,128)S(1)} %fusion.48), custom_call_target="InvertDiagBlocksLowerTriangular" | custom-call | tf_op jit(solution)/shard_map/jit(_solve_triangular)/triangular_solve | solution.py:29
  86.8 1.8 fusion.18
  88.6 0.4 fusion.77
  89.0 4.5 %convolution_bitcast_fusion = f32[1024,1280]{1,0:T(8,128)S(1)} fusion(f32[44,1280]{1,0:T(8,128)S(1)} %fusion.77, f32[44,1024]{1,0:T(8,128)S(1)} %copy-done), kind=kOutput, calls=%fused_computation.9 | convolution fusion | flops 692060160 | bytes 5648384 | tf_op jit(solution)/shard_map/cs,cp->sp/dot_general | solution.py:37
  93.6 0.9 multiply_reduce_fusion
  94.5 1.4 copy-done.1
  95.9 7.2 %fusion.5 = bf16[3072,1024]{1,0:T(8,128)(2,1)S(1)} fusion(bf16[1024,1024]{1,0:T(8,128)(2,1)S(1)} %get-tuple-element.3, s32[1024]{0:T(1024)S(1)} %iota_add_fusion, s32[3072]{0:T(1024)S(1)} %eq.77), kind=kOutput, calls=%fused_computation.8 | convolution fusion | flops 6448742400 | bytes 8404992 | tf_op jit(solution)/shard_map/dot_general | solution.py:56
  103.0 3.4 %copy.34 = bf16[4,16,48,1024]{3,2,0,1:T(8,128)(2,1)} copy(bf16[4,16,48,1024]{3,2,1,0:T(8,128)(2,1)S(1)} %bitcast.104) | data formatting | bytes 12582912 | tf_op jit(solution)/shard_map/reshape | solution.py:60
  106.4 7.3 %all-to-all-start = ((bf16[4,16,48,1024]{3,2,0,1:T(8,128)(2,1)}), bf16[4,16,48,1024]{3,2,0,1:T(8,128)(2,1)}, u32[]{:S(2)}, u32[]{:S(2)}) async-start(bf16[4,16,48,1024]{3,2,0,1:T(8,128)(2,1)} %copy.34), calls=%async_computation.1 | async-start | bytes 12582912 | tf_op jit(solution)/shard_map/all_to_all | solution.py:59
  114.3 2.8 convolution_convert_fusion.1
  117.2 111.2 %all-to-all-done = bf16[4,16,48,1024]{3,2,0,1:T(8,128)(2,1)} async-done(((bf16[4,16,48,1024]{3,2,0,1:T(8,128)(2,1)}), bf16[4,16,48,1024]{3,2,0,1:T(8,128)(2,1)}, u32[]{:S(2)}, u32[]{:S(2)}) %all-to-all-start) | async-done | bytes 6291488 | tf_op jit(solution)/shard_map/all_to_all | solution.py:59
  228.4 3.5 %copy.35 = bf16[4,16,48,1024]{3,2,1,0:T(8,128)(2,1)S(1)} copy(bf16[4,16,48,1024]{3,2,0,1:T(8,128)(2,1)} %all-to-all-done) | data formatting | bytes 12582912 | tf_op jit(solution)/shard_map/all_to_all | solution.py:59
  231.9 3.8 %fusion.10 = bf16[4,512,1024]{2,1,0:T(8,128)(2,1)S(1)} fusion(bf16[4,768,1024]{2,1,0:T(8,128)(2,1)S(1)} %bitcast.105, s32[4,512]{1,0:T(4,128)S(1)} %fusion.55), kind=kOutput, calls=%fused_computation.14 | convolution fusion | flops 3224895488 | bytes 10493952 | tf_op jit(solution)/shard_map/sjk,skr->sjr/dot_general | solution.py:103
  235.7 2.1 convolution_convert_fusion
  237.7 1.4 multiply_reduce_fusion.1
  239.2 8.4 %psum.15 = f32[1280]{0:T(1024)S(1)} all-reduce(f32[1280]{0:T(1024)S(1)} %pad_maximum_fusion.1), channel_id=1, replica_groups=mesh['sample'=4,'variant'=16,'protein'=8] {'sample'}, use_global_device_ids=true, to_apply=%region_6.7 | all-reduce | flops 1280 | bytes 10240 | tf_op jit(solution)/shard_map/psum | solution.py:76
  247.7 1.0 multiply_convert_fusion
  248.7 10.8 %all_gather.3 = bf16[1024,256]{1,0:T(8,128)(2,1)S(1)} all-gather(bf16[256,256]{1,0:T(8,128)(2,1)S(1)} %multiply_convert_fusion), channel_id=1, replica_groups=mesh['sample'=4,'variant'=16,'protein'=8] {'sample'}, dimensions={0}, use_global_device_ids=true | all-gather | bytes 655360 | tf_op jit(solution)/shard_map/all_gather | solution.py:82
  259.5 1.0 convert_element_type.67
  260.5 26.6 %reduce-scatter.5.cloned.1.call-done = bf16[1,4,128,128]{3,2,1,0:T(8,128)(2,1)} async-done(((bf16[4,4,128,128]{3,2,1,0:T(8,128)(2,1)}), bf16[1,4,128,128]{3,2,1,0:T(8,128)(2,1)}) %reduce-scatter.5.cloned.1.call-update) | async-done | bytes 131088 | tf_op jit(solution)/shard_map/reduce_scatter | solution.py:108
  287.2 1.6 multiply_bitcast_fusion
  (40 shorter events, 2.1 us)
Async XLA Ops:
  7.2 0.9 copy-start
  7.2 6.6 %copy-start.5 = (s32[64,4]{0,1:T(4,128)S(1)}, s32[64,4]{0,1:T(4,128)}, u32[]{:S(2)}) copy-start(s32[64,4]{0,1:T(4,128)} %param.9) | copy-start | bytes 3076
  7.2 6.7 %copy-start.4 = (s32[64,4,128]{2,1,0:T(4,128)S(1)}, s32[64,4,128]{2,1,0:T(4,128)}, u32[]{:S(2)}) copy-start(s32[64,4,128]{2,1,0:T(4,128)} %param.8) | copy-start | bytes 393220
  7.2 69.0 %all-reduce.2.cloned.1.call-start = ((), (), s32[]{:S(2)}) async-start(), calls=%async_computation.3 | async-start | bytes 1359872 | tf_op jit(solution)/shard_map/psum | solution.py:26
  89.0 4.6 %copy-start.2 = (bf16[1024,1024]{1,0:T(8,128)(2,1)S(1)}, bf16[1024,1024]{1,0:T(8,128)(2,1)}, u32[]{:S(2)}) copy-start(bf16[1024,1024]{1,0:T(8,128)(2,1)} %param.5) | copy-start | bytes 6291460
  93.6 2.3 copy-start.1
  106.4 7.9 %copy-start.3 = (bf16[1024,256]{1,0:T(8,128)(2,1)S(1)}, bf16[1024,256]{1,0:T(8,128)(2,1)}, u32[]{:S(2)}) copy-start(bf16[1024,256]{1,0:T(8,128)(2,1)} %param.6) | copy-start | bytes 1572868
  106.4 122.0 %all-to-all-start = ((bf16[4,16,48,1024]{3,2,0,1:T(8,128)(2,1)}), bf16[4,16,48,1024]{3,2,0,1:T(8,128)(2,1)}, u32[]{:S(2)}, u32[]{:S(2)}) async-start(bf16[4,16,48,1024]{3,2,0,1:T(8,128)(2,1)} %copy.34), calls=%async_computation.1 | async-start | bytes 12582912 | tf_op jit(solution)/shard_map/all_to_all | solution.py:59
  113.7 134.0 %reduce-scatter.3.cloned.1.call-start = ((), (), s32[]{:S(2)}) async-start(), calls=%async_computation.4 | async-start | bytes 655360 | tf_op jit(solution)/shard_map/reduce_scatter | solution.py:78
  117.1 170.1 %reduce-scatter.5.cloned.1.call-start = ((), (), s32[]{:S(2)}) async-start(), calls=%async_computation.5 | async-start | bytes 655360 | tf_op jit(solution)/shard_map/reduce_scatter | solution.py:108
Sparse Core Ops, SparseCore 0:
  13.9 62.2 all-reduce.1
  118.1 28.7 reduce-scatter.2
  237.9 49.2 reduce-scatter.4

commit v2 on v1

v2 whole, which is shorter than its diff:
```python
import functools

import jax
import jax.numpy as jnp
from jax import lax
from jax.experimental import pallas as pl
from jax.experimental.pallas import tpu as pltpu
from jax.sharding import PartitionSpec as P

BF16 = jnp.bfloat16
F32 = jnp.float32
MESH = pl.DeviceIdType.MESH
BEST = lax.Precision.HIGHEST
NT = (((1,), (1,)), ((), ()))
CHUNKS = 4
CP = 48
CB = 64


def kernel(n_z, n_cov, cap, freedom, dos, prot, cf, c3, ct, col, pos, z_out, g_out, *scratch):
    (
        dall, d2own, d2c, pick, out, rec, fr, fl, arb, bt, bc, prt, ssend, srecv, auxb, auxs, zbuf,
        gacc, gsend, grecv, *sems,
    ) = scratch
    ag, fw, sw, bag, bfw, bsw, ar, sc, ax, zg, gr, yd, yf, yg = zip(sems[0::2], sems[1::2])

    x = lax.axis_index("sample")
    v = lax.axis_index("variant")
    q = lax.axis_index("protein")
    y, zl = lax.rem(v, 4), v // 4
    core, zh = lax.rem(q, 2), q // 2
    z = zh * 4 + zl

    def at_x(d):
        return (lax.rem(x + d, 4), v, q)

    def at_y(d):
        return (x, zl * 4 + lax.rem(y + d, 4), q)

    def at_z(d):
        there = lax.rem(z + d + n_z, n_z)
        return (x, lax.rem(there, 4) * 4 + y, (there // 4) * 2 + core)

    right, left, sibling = at_z(1), at_z(-1), (x, v, zh * 2 + 1 - core)
    up, down = at_y(1), at_y(3)

    neighbours = [at_x(1), at_x(2), at_x(3), up, down, right, left, sibling]
    barrier = pltpu.get_barrier_semaphore()
    for there in neighbours:
        pl.semaphore_signal(barrier, inc=1, device_id=there, device_id_type=MESH)
    pl.semaphore_wait(barrier, len(neighbours))

    sent = []

    def send(src, dst, sem, at, there):
        copy = pltpu.make_async_remote_copy(
            src_ref=src,
            dst_ref=dst,
            send_sem=sem[0].at[at],
            recv_sem=sem[1].at[at],
            device_id=there,
            device_id_type=MESH,
        )
        copy.start()
        sent.append(copy)
        return copy

    rows, v_dev = dos.shape
    n_prot = prot.shape[1]
    crows = rows // CHUNKS
    half = crows // 2
    quarter = half // 2
    wide = v_dev // 2
    mine = pl.multiple_of(core * half, half)
    copies = {}

    def piece(k, more=0, size=half):
        return pl.ds(pl.multiple_of(k * crows + core * half + more, quarter), size)

    def gather_own(k):
        part = dos.at[piece(k)]
        copies["a", k] = send(part, dall.at[0, piece(k)], ag, (k, 0), right)
        copies["b", k] = send(part, dall.at[2, piece(k)], ag, (k, 1), left)

    def gather_on(k):
        high, low = piece(k, quarter, quarter), piece(k, 0, quarter)
        copies["a", k].wait_recv()
        copies["c", k] = send(dall.at[0, high], dall.at[1, high], fw, (k, 0), right)
        copies["s0", k] = send(dall.at[0, piece(k)], dall.at[0, piece(k)], sw, (k, 0), sibling)
        copies["b", k].wait_recv()
        copies["d", k] = send(dall.at[2, low], dall.at[1, low], fw, (k, 1), left)
        copies["s2", k] = send(dall.at[2, piece(k)], dall.at[2, piece(k)], sw, (k, 2), sibling)

    def gather_far(k):
        copies["c", k].wait_recv()
        copies["d", k].wait_recv()
        copies["s1", k] = send(dall.at[1, piece(k)], dall.at[1, piece(k)], sw, (k, 1), sibling)

    gather_own(0)
    gather_own(1)

    ours = pl.multiple_of(core * wide, wide)
    c3v = c3[...]
    cd = jnp.dot(c3v, dos[:, pl.ds(ours, wide)], preferred_element_type=F32)
    cq = jnp.dot(c3v, prot[...], preferred_element_type=F32)
    cc = lax.dot_general(cf[...], cf[...], NT, precision=BEST, preferred_element_type=F32)
    arb[x, :, 0:wide] = cd[0:CP] + cd[CP : 2 * CP] + cd[2 * CP :]
    arb[x, :, wide : wide + n_prot] = cq[0:CP] + cq[CP : 2 * CP] + cq[2 * CP :]
    arb[x, :, wide + n_prot :] = jnp.zeros((CP, 128), F32)
    arb[x, :, wide + n_prot : wide + n_prot + CP] = cc
    sums = [send(arb.at[x], arb.at[x], ar, d - 1, at_x(d)) for d in (1, 2, 3)]

    tile = 512
    per_row = 4 * v_dev // tile

    def build(step, carry):
        row, part = step // per_row, lax.rem(step, per_row)
        places = lax.broadcasted_iota(jnp.int32, (4 * cap, tile), 1) + (part * tile + 1)
        hit = jnp.where(col[row] == places, 1.0, 0.0).astype(BF16)
        pick[row, :, pl.ds(pl.multiple_of(part * tile, tile), tile)] = hit
        return carry

    lax.fori_loop(0, 4 * per_row, build, 0)

    gather_on(0)
    gather_own(2)

    for copy in sums:
        copy.wait_recv()
    total = arb[0] + arb[1] + arb[2] + arb[3]
    lane = lax.broadcasted_iota(jnp.int32, (CP, 128), 1)
    row = lax.broadcasted_iota(jnp.int32, (CP, 128), 0)
    both = total[:, wide + n_prot :]
    both = both + jnp.where((lane == row) & (row >= n_cov), 1.0, 0.0)
    both = both + jnp.where(lane == row + 64, 1.0, 0.0)
    unit = lax.broadcasted_iota(jnp.int32, (CP, 1), 0)
    for i in range(n_cov):
        scaled = both[i : i + 1, :] / both[i : i + 1, i : i + 1]
        both = both - (both[:, i : i + 1] - jnp.where(unit == i, 1.0, 0.0)) * scaled
    inverse = pltpu.roll(both, 64, 1)[:, 0:CP]
    coef = jnp.dot(
        inverse, total[:, : wide + n_prot], precision=BEST, preferred_element_type=F32
    )

    bt[0, core, 0:CP, :] = coef[:, :wide].astype(BF16)
    bt[0, core, CP:CB, :] = jnp.zeros((CB - CP, wide), BF16)
    low, high = pl.ds(0, CB // 2), pl.ds(CB // 2, CB // 2)
    b_a = send(bt.at[0, core], bt.at[1, core], bag, 0, right)
    b_b = send(bt.at[0, core], bt.at[3, core], bag, 1, left)
    b_s = [send(bt.at[0, core], bt.at[0, core], bsw, 0, sibling)]

    gather_on(1)
    gather_own(3)
    gather_far(0)

    cb = coef[:, wide:]
    ch = cb.astype(BF16)
    cm = (cb - ch.astype(F32)).astype(BF16)
    gap = jnp.zeros((CB - CP, n_prot), BF16)
    ctv = ct[...]
    fit = jnp.dot(ctv, jnp.concatenate([ch, gap, ch, gap]), preferred_element_type=F32)
    fit = fit + jnp.dot(ctv, jnp.concatenate([cm, gap, cm, gap]), preferred_element_type=F32)
    res = (prot[...].astype(F32) - fit).astype(BF16).astype(F32)
    auxb[x, :, v_dev:] = jnp.broadcast_to(
        jnp.sum(res * res, axis=0, keepdims=True), (8, n_prot)
    )
    prt[...] = res.T.astype(BF16)

    b_a.wait_recv()
    b_c = send(bt.at[1, core, high], bt.at[2, core, high], bfw, 0, right)
    b_s.append(send(bt.at[1, core], bt.at[1, core], bsw, 1, sibling))
    b_b.wait_recv()
    b_d = send(bt.at[3, core, low], bt.at[2, core, low], bfw, 1, left)
    b_s.append(send(bt.at[3, core], bt.at[3, core], bsw, 2, sibling))

    def stack(slot):
        for side in range(2):
            part = bt[slot, side]
            bc[slot, 0:CB, side * wide : (side + 1) * wide] = part
            bc[slot, CB:, side * wide : (side + 1) * wide] = part

    b_s[0].wait_recv()
    stack(0)

    def own_residual(k, squares):
        here = pl.ds(pl.multiple_of(k * crows, crows), crows)
        fit = jnp.dot(ct[here, :], bc[0], preferred_element_type=F32)
        res = dos[here, :].astype(F32) - fit
        d2own[here, :] = res.astype(BF16)
        return squares + jnp.sum(res * res, axis=0, keepdims=True)

    squares = lax.fori_loop(0, CHUNKS, own_residual, jnp.zeros((1, v_dev), F32))
    auxb[x, :, :v_dev] = jnp.broadcast_to(squares, (8, v_dev))
    own = v_dev // 4

    def score(i, carry):
        cols = pl.ds(pl.multiple_of(i * own, own), own)
        ssend[i] = jnp.dot(prt[...], d2own[:, cols], preferred_element_type=F32).astype(BF16)
        return carry

    lax.fori_loop(0, 4, score, 0)
    s_c = [
        send(ssend.at[lax.rem(x + d, 4)], srecv.at[d - 1], sc, d - 1, at_x(d)) for d in (1, 2, 3)
    ]
    a_c = [send(auxb.at[x], auxb.at[x], ax, d - 1, at_x(d)) for d in (1, 2, 3)]

    gather_on(2)
    gather_far(1)
    b_c.wait_recv()
    b_d.wait_recv()
    b_s.append(send(bt.at[2, core], bt.at[2, core], bsw, 3, sibling))
    for copy in b_s[1:]:
        copy.wait_recv()
    for slot in (1, 2, 3):
        stack(slot)

    def choose(k):
        here = pl.ds(k * crows, crows)
        for slot in range(3):
            copies["s%d" % slot, k].wait_recv()
            fit = jnp.dot(ct[here, :], bc[slot + 1], preferred_element_type=F32)
            d2c[slot] = (dall[slot, here, :].astype(F32) - fit).astype(BF16)

        def one(to, carry):
            part = lax.dot_general(
                pick[to, :, 0:v_dev], d2own[here, :], NT, preferred_element_type=F32
            )
            for slot in range(3):
                part = part + lax.dot_general(
                    pick[to, :, (slot + 1) * v_dev : (slot + 2) * v_dev],
                    d2c[slot],
                    NT,
                    preferred_element_type=F32,
                )
            out[k, to] = part.astype(BF16)
            return carry

        lax.fori_loop(0, 4, one, 0)
        ahead, behind, across = lax.rem(y + 1, 4), lax.rem(y + 3, 4), lax.rem(y + 2, 4)
        first, second = pl.ds(0, 2 * cap), pl.ds(2 * cap, 2 * cap)
        copies["f0", k] = send(out.at[k, across, first], fr.at[k], yf, (k, 0), up)
        copies["f1", k] = send(out.at[k, across, second], fl.at[k], yf, (k, 1), down)
        copies["y0", k] = send(out.at[k, ahead], rec.at[k, y], yd, (k, 0), up)
        copies["y1", k] = send(out.at[k, behind], rec.at[k, y], yd, (k, 1), down)
        rec[k, y] = out[k, y]

    def pass_on(k):
        ahead, behind = lax.rem(y + 1, 4), lax.rem(y + 3, 4)
        first, second = pl.ds(0, 2 * cap), pl.ds(2 * cap, 2 * cap)
        copies["f0", k].wait_recv()
        copies["g0", k] = send(fr.at[k], rec.at[k, behind, first], yg, (k, 0), up)
        copies["f1", k].wait_recv()
        copies["g1", k] = send(fl.at[k], rec.at[k, ahead, second], yg, (k, 1), down)

    def gram(k):
        for name in ("y0", "y1", "g0", "g1"):
            copies[name, k].wait_recv()

        def one(to, carry):
            lines = pl.ds(pl.multiple_of(to * cap, cap), cap)
            got = jnp.concatenate([rec[k, i, lines, :] for i in range(4)])
            places = lax.broadcasted_iota(jnp.int32, (4 * 128, 4 * cap), 1)
            place = jnp.where(pos[to] == places, 1.0, 0.0).astype(BF16)
            hits = jnp.dot(place, got, preferred_element_type=F32).astype(BF16)
            for p in range(4):
                h = hits[p * 128 : (p + 1) * 128]
                g = lax.dot_general(h, h, NT, preferred_element_type=F32)
                if k == 0:
                    gacc[to, p] = g
                else:
                    gacc[to, p] = gacc[to, p] + g
            return carry

        lax.fori_loop(0, 4, one, 0)

    choose(0)

    for copy in s_c + a_c:
        copy.wait_recv()
    auxs[...] = auxb[0] + auxb[1] + auxb[2] + auxb[3]
    quarter_v = pl.ds(pl.multiple_of(x * own, own), own)
    dos_var = auxs[0:1, quarter_v]
    rss = auxs[0:1, v_dev:]
    whole = ssend[x].astype(F32)
    for d in range(3):
        whole = whole + srecv[d].astype(F32)
    whole = (whole / jnp.sqrt(dos_var)).T / jnp.sqrt(rss / freedom + 1e-05)
    zbuf[quarter_v, :] = whole.astype(BF16)
    z_c = [send(zbuf.at[quarter_v], zbuf.at[quarter_v], zg, d - 1, at_x(d)) for d in (1, 2, 3)]

    gather_on(3)
    gather_far(2)
    choose(1)
    pass_on(0)
    gather_far(3)
    choose(2)
    pass_on(1)
    gram(0)
    choose(3)
    pass_on(2)
    gram(1)
    pass_on(3)
    gram(2)
    for copy in z_c:
        copy.wait_recv()
    z_out[...] = zbuf[...]
    gram(3)
    gsend[...] = gacc[...].astype(BF16)
    g_c = [
        send(gsend.at[lax.rem(x + d, 4)], grecv.at[d - 1], gr, d - 1, at_x(d)) for d in (1, 2, 3)
    ]
    whole = gacc[x]
    for d in range(3):
        g_c[d].wait_recv()
        whole = whole + grecv[d].astype(F32)
    g_out[...] = whole
    for copy in sent:
        copy.wait_send()


def shards(n_z, dosages, proteins, covariates, hit_index, hit_count):
    n_sample = lax.axis_size("sample")
    n_variant = lax.axis_size("variant")
    rows, v_dev = dosages.shape
    n_prot = proteins.shape[1]
    n_cov = covariates.shape[0]
    samples = rows * n_sample
    n_dest, p_own, slots = hit_index.shape
    flat = p_own * slots
    block_hits = max(p_own * 16, 2 * slots)
    most = 3 * block_hits // n_variant
    other = -(-(block_hits - most) // (n_variant - 1))
    cap = -(-(most + 3 * other) // 16) * 16
    v = lax.axis_index("variant")
    y, zl = lax.rem(v, 4), v // 4

    lists = hit_index.reshape(n_sample, 4, 4, flat)
    lists = lax.dynamic_index_in_dim(lists, zl, 1, keepdims=False).transpose(1, 0, 2)
    slot_ids = jnp.arange(slots, dtype=jnp.int32)
    live = slot_ids < lax.dynamic_index_in_dim(
        hit_count.reshape(n_sample, 4, 4, p_own), zl, 1, keepdims=False
    ).transpose(1, 0, 2)[..., None]
    live = live.reshape(4, n_sample, flat)
    block = lists // v_dev
    upper = jnp.triu(jnp.ones((flat, flat), BF16))

    chosen = live & (block % 4 == y)
    rank = jnp.dot(chosen.astype(BF16), upper, preferred_element_type=F32).astype(jnp.int32) - 1
    rank = jnp.where(chosen, rank, -1)
    column = lists - block * v_dev + ((zl - block // 4) % 4) * v_dev + 1
    places = jnp.arange(cap, dtype=jnp.int32)
    col = jnp.sum(
        jnp.where(rank[:, :, None, :] == places[:, None], column[:, :, None, :], 0), axis=3
    ).reshape(4, n_sample * cap, 1)

    own_live = lax.dynamic_index_in_dim(live, y, 0, keepdims=False)
    own_line = lax.dynamic_index_in_dim(block, y, 0, keepdims=False) % 4
    member = own_live[:, None, :] & (own_line[:, None, :] == jnp.arange(4)[:, None])
    upto = jnp.dot(member.astype(BF16), upper, preferred_element_type=F32)
    rank_in = jnp.sum(jnp.where(member, upto, 0.0), axis=1).astype(jnp.int32) - 1
    pos = jnp.where(own_live, own_line * cap + rank_in, -1).reshape(n_sample, flat, 1)

    cf = jnp.pad(covariates, ((0, CP - n_cov), (0, 0)))
    part = lax.reduce_precision(cf, 8, 7)
    rest = cf - part
    middle = lax.reduce_precision(rest, 8, 7)
    last = rest - middle
    c3 = jnp.concatenate([part, middle, last]).astype(BF16)
    gap = jnp.zeros((CB - CP, rows), F32)
    ct = jnp.concatenate([part, gap, middle, gap]).T.astype(BF16)

    def vmem(shape, dtype=BF16):
        return pltpu.VMEM(shape, dtype)

    def pair(shape):
        return [pltpu.SemaphoreType.DMA(shape)] * 2

    crows = rows // CHUNKS
    own = v_dev // 4
    scratch = [
        vmem((3, rows, v_dev)),
        vmem((rows, v_dev)),
        vmem((3, crows, v_dev)),
        vmem((4, 4 * cap, 4 * v_dev)),
        vmem((CHUNKS, 4, 4 * cap, crows)),
        vmem((CHUNKS, 4, 4 * cap, crows)),
        vmem((CHUNKS, 2 * cap, crows)),
        vmem((CHUNKS, 2 * cap, crows)),
        vmem((4, CP, v_dev // 2 + n_prot + 128), F32),
        vmem((4, 2, CB, v_dev // 2)),
        vmem((4, 2 * CB, v_dev)),
        vmem((n_prot, rows)),
        vmem((4, n_prot, own)),
        vmem((3, n_prot, own)),
        vmem((4, 8, v_dev + n_prot), F32),
        vmem((8, v_dev + n_prot), F32),
        vmem((v_dev, n_prot)),
        vmem((4, p_own, slots, slots), F32),
        vmem((4, p_own, slots, slots)),
        vmem((3, p_own, slots, slots)),
        *pair((CHUNKS, 2)),
        *pair((CHUNKS, 2)),
        *pair((CHUNKS, 3)),
        *pair((2,)),
        *pair((2,)),
        *pair((4,)),
        *pair((3,)),
        *pair((3,)),
        *pair((3,)),
        *pair((3,)),
        *pair((3,)),
        *pair((CHUNKS, 2)),
        *pair((CHUNKS, 2)),
        *pair((CHUNKS, 2)),
    ]
    z, g = pl.pallas_call(
        functools.partial(kernel, n_z, n_cov, cap, float(samples - n_cov)),
        out_shape=(
            jax.ShapeDtypeStruct((v_dev, n_prot), BF16),
            jax.ShapeDtypeStruct((p_own, slots, slots), F32),
        ),
        in_specs=[pl.BlockSpec(memory_space=pltpu.VMEM)] * 7,
        out_specs=(pl.BlockSpec(memory_space=pltpu.VMEM),) * 2,
        scratch_shapes=scratch,
        compiler_params=pltpu.CompilerParams(
            collective_id=0, has_side_effects=True, vmem_limit_bytes=58 * 1024 * 1024
        ),
    )(dosages, proteins, cf, c3, ct, col, pos)
    return (z.astype(F32), g / F32(samples))


def solution(mesh):
    in_specs = (
        P("sample", "variant"),
        P("sample", "protein"),
        P(None, "sample"),
        P(None, "protein", None),
        P(None, "protein"),
    )
    out_specs = (P("variant", "protein"), P(("sample", "variant", "protein"), None, None))
    n_z = 4 * (mesh.shape["protein"] // 2)
    return jax.shard_map(
        functools.partial(shards, n_z),
        mesh=mesh,
        in_specs=in_specs,
        out_specs=out_specs,
        check_vma=False,
    )
```

time: 297 us -> 123 us (0.41)
  waiting for transfers between devices: 199 us -> 0 us
  Pallas kernels: 0 us -> 107 us
  matrix products: 27.9 us -> 0.65 us
  blocking collectives: 19.2 us -> 0 us
  between operations: 14.1 us -> 0.82 us
  other arithmetic: 16.8 us -> 7.44 us
  starting transfers between devices: 7.38 us -> 0 us
  local copies, waits for them, and re-layouts: 11.5 us -> 6.87 us
    all_to_all x1 -> x0, waiting for transfers between devices: 111 us -> none  [shards(): lax.all_to_all(outgoing.reshape(n_sample, n_variant, capacity, rows), 'va...]
    pallas_call x0 -> x1, Pallas kernels: none -> 107 us  [shards(): pl.pallas_call(functools.partial(kernel, n_z, n_cov, cap, float(samples -...]
    psum x1 -> x0, waiting for transfers between devices: 60.6 us -> none  [shards(): lax.psum(jnp.concatenate([dos_part, prot_part, gram_part], axis=1), 'samp...]
    dot_general x11 -> x1, matrix products: 27.3 us -> 0.33 us  [shards(): upto = jnp.dot(member.astype(BF16), upper, preferred_element_type=F32)]
    reduce_scatter x2 -> x0, waiting for transfers between devices: 26.7 us -> none  [the longest x1 26.6 us: shards(): lax.psum_scatter(gram.astype(BF16), 'sample', scatter_dimension=0, tiled=...]
    all_gather x1 -> x0, blocking collectives: 10.8 us -> none  [shards(): lax.all_gather(z.astype(BF16), 'sample', axis=0, tiled=True).astype(F32)]
    another operation x5 -> x1, other arithmetic: 8.7 us -> 0.14 us  [the longest x3 4.68 us: shards(): factor = jnp.linalg.cholesky(gram_cov)]
    psum x1 -> x0, blocking collectives: 8.39 us -> none  [shards(): squares = lax.psum(squares, 'sample')]
  transfers between devices with their start and end apart: 4 -> 0, of which waited for: 3 -> 0; matrix products, arithmetic and copies ran while one was open for 6% -> 0% of each run, Pallas kernels for 0% -> 0%
where the time goes in v2:
time: 123 us
  Pallas kernels  107 us (87%)
  other arithmetic  7.44 us (6%)
  local copies, waits for them, and re-layouts  6.87 us (6%)
    pallas_call x1, Pallas kernels, shards(): pl.pallas_call(functools.partial(kernel, n_z, n_cov, cap, float(samples -...  107 us

profile of v2, /device:TPU:1, one launch (start us, length us, event | category | flops | bytes accessed | tf_op | source)
XLA Modules:
  0.0 122.9 jit_solution(832830079834874144)
XLA Ops:
  0.7 1.0 reshape.125
  1.7 0.1 fusion.24
  1.8 0.8 reshape.124
  2.6 0.1 copy.51
  2.7 0.1 lt.54
  2.9 0.3 fusion.2
  3.3 0.4 copy.44
  3.6 0.4 copy.41
  4.0 0.5 copy.45
  4.5 0.0 copy-start
  4.5 1.5 %fusion.6.pos = s32[4,512,1]{2,1,0:T(8,128)} fusion(pred[4,512,1]{2,1,0:T(8,128)(4,1)S(1)} %copy.45, s32[4,512,1]{2,1,0:T(8,128)S(1)} %copy.44, s32[4,512,1]{2,1,0:T(8,128)S(1)} %copy.41), kind=kLoop, calls=%fused_computation.13 | loop fusion | flops 28672 | bytes 26624 | tf_op jit(solution)/shard_map/jit(_where)/select_n | solution.py:361
  6.0 0.3 fusion.1
  6.4 0.4 select_reduce_fusion
  6.8 1.6 %reshape.128.col = s32[4,384,1]{2,1,0:T(8,128)} reshape(s32[4,4,96]{2,1,0:T(4,128)S(1)} %select_reduce_fusion) | data formatting | bytes 12288 | tf_op jit(solution)/shard_map/reshape | solution.py:354
  8.3 0.0 copy-done
  8.4 0.2 copy.37
  8.6 0.1 reduce-precision_convert_fusion.1
  8.7 0.4 pad_maximum_fusion
  9.1 0.9 copy.47.c3
  10.1 1.0 maximum_bitcast_fusion.ct
  11.1 0.2 copy.57
  11.3 0.7 pad.4.clone.cf
  12.0 107.2 %shard_map.68 = (bf16[1024,256]{1,0:T(8,128)(2,1)}, f32[4,128,128]{2,1,0:T(8,128)}) custom-call(bf16[1024,1024]{1,0:T(8,128)(2,1)} %dos.1, bf16[1024,256]{1,0:T(8,128)(2,1)} %prot.1, f32[48,1024]{1,0:T(8,128)} %pad.4.clone.cf, bf16[144,1024]{1,0:T(8,128)(2,1)} %copy.47.c3, bf16[1024,128]{1,0:T(8,128)(2,1)} %maximum_bitcast_fusion.ct, ...), custom_call_target="tpu_custom_call" | custom-call | tf_op jit(solution)/shard_map/pallas_call | solution.py:416
  119.2 2.1 %convert_element_type.28 = f32[1024,256]{1,0:T(8,128)} convert(bf16[1024,256]{1,0:T(8,128)(2,1)} %get-tuple-element.4) | non-fusion elementwise | flops 262144 | bytes 1572864 | tf_op jit(solution)/shard_map/convert_element_type | solution.py:429
  121.3 1.7 %broadcast_multiply_fusion = f32[4,128,128]{2,1,0:T(8,128)} fusion(f32[4,128,128]{2,1,0:T(8,128)} %get-tuple-element.5), kind=kLoop, calls=%fused_computation.30 | loop fusion | flops 65536 | bytes 524288 | tf_op jit(solution)/shard_map/div | solution.py:429
  (11 shorter events, 0.2 us)
Async XLA Ops:
  4.5 3.8 %copy-start = (f32[44,1024]{1,0:T(8,128)S(1)}, f32[44,1024]{1,0:T(8,128)}, u32[]{:S(2)}) copy-start(f32[44,1024]{1,0:T(8,128)} %param.7) | copy-start | bytes 540676

commit v3 on v2

v3 whole, which is shorter than its diff:
```python
import functools

import jax
import jax.numpy as jnp
from jax import lax
from jax.experimental import pallas as pl
from jax.experimental.pallas import tpu as pltpu
from jax.sharding import PartitionSpec as P

BF16 = jnp.bfloat16
F32 = jnp.float32
MESH = pl.DeviceIdType.MESH
BEST = lax.Precision.HIGHEST
NT = (((1,), (1,)), ((), ()))
CHUNKS = 4
CP = 48
CB = 64


def kernel(n_z, n_cov, cap, freedom, dos, prot, cov, hidx, hcnt, z_out, g_out, *scratch):
    (
        dall, d2own, pick, out, rec, fr, fl, arb, bt, bc, prt, ssend, srecv, auxb, auxs, zbuf,
        gacc, gsend, grecv, cf, ct, c2, ranks, places, slot_pos, lows, highs, place,
        bout, brec, bfr, bfl, bsel, *sems,
    ) = scratch
    ag, fw, sw, bag, bfw, bsw, ar, sc, ax, zg, gr, yd, yf, yg, hd, hf, hg = zip(sems[0::2], sems[1::2])

    x = lax.axis_index("sample")
    v = lax.axis_index("variant")
    q = lax.axis_index("protein")
    y, zl = lax.rem(v, 4), v // 4
    core, zh = lax.rem(q, 2), q // 2
    z = zh * 4 + zl

    def at_x(d):
        return (lax.rem(x + d, 4), v, q)

    def at_y(d):
        return (x, zl * 4 + lax.rem(y + d, 4), q)

    def at_z(d):
        there = lax.rem(z + d + n_z, n_z)
        return (x, lax.rem(there, 4) * 4 + y, (there // 4) * 2 + core)

    right, left, sibling = at_z(1), at_z(-1), (x, v, zh * 2 + 1 - core)
    up, down = at_y(1), at_y(3)

    neighbours = [at_x(1), at_x(2), at_x(3), up, down, right, left, sibling]
    barrier = pltpu.get_barrier_semaphore()
    for there in neighbours:
        pl.semaphore_signal(barrier, inc=1, device_id=there, device_id_type=MESH)
    pl.semaphore_wait(barrier, len(neighbours))

    sent = []

    def send(src, dst, sem, at, there):
        copy = pltpu.make_async_remote_copy(
            src_ref=src,
            dst_ref=dst,
            send_sem=sem[0].at[at],
            recv_sem=sem[1].at[at],
            device_id=there,
            device_id_type=MESH,
        )
        copy.start()
        sent.append(copy)
        return copy

    rows, v_dev = dos.shape
    n_prot = prot.shape[1]
    slots = hidx.shape[2]
    crows = rows // CHUNKS
    half = crows // 2
    quarter = half // 2
    wide = v_dev // 2
    mine = pl.multiple_of(core * half, half)
    copies = {}

    def piece(k, more=0, size=half):
        return pl.ds(pl.multiple_of(k * crows + core * half + more, quarter), size)

    def gather_own(k):
        part = dos.at[piece(k)]
        copies["a", k] = send(part, dall.at[0, piece(k)], ag, (k, 0), right)
        copies["b", k] = send(part, dall.at[2, piece(k)], ag, (k, 1), left)

    def gather_on(k):
        high, low = piece(k, quarter, quarter), piece(k, 0, quarter)
        copies["a", k].wait_recv()
        copies["c", k] = send(dall.at[0, high], dall.at[1, high], fw, (k, 0), right)
        copies["s0", k] = send(dall.at[0, piece(k)], dall.at[0, piece(k)], sw, (k, 0), sibling)
        copies["b", k].wait_recv()
        copies["d", k] = send(dall.at[2, low], dall.at[1, low], fw, (k, 1), left)
        copies["s2", k] = send(dall.at[2, piece(k)], dall.at[2, piece(k)], sw, (k, 2), sibling)

    def gather_far(k):
        copies["c", k].wait_recv()
        copies["d", k].wait_recv()
        copies["s1", k] = send(dall.at[1, piece(k)], dall.at[1, piece(k)], sw, (k, 1), sibling)

    def choose(k):
        here = pl.ds(k * crows, crows)
        for slot in range(3):
            copies["s%d" % slot, k].wait_recv()

        def one(to, carry):
            part = lax.dot_general(
                pick[to, :, 0:v_dev], dos[here, :], NT, preferred_element_type=F32
            )
            for slot in range(3):
                part = part + lax.dot_general(
                    pick[to, :, (slot + 1) * v_dev : (slot + 2) * v_dev],
                    dall[slot, here, :],
                    NT,
                    preferred_element_type=F32,
                )
            out[k, to] = part.astype(BF16)
            return carry

        lax.fori_loop(0, 4, one, 0)
        ahead, behind, across = lax.rem(y + 1, 4), lax.rem(y + 3, 4), lax.rem(y + 2, 4)
        first, second = pl.ds(0, 2 * cap), pl.ds(2 * cap, 2 * cap)
        copies["f0", k] = send(out.at[k, across, first], fr.at[k], yf, (k, 0), up)
        copies["f1", k] = send(out.at[k, across, second], fl.at[k], yf, (k, 1), down)
        copies["y0", k] = send(out.at[k, ahead], rec.at[k, y], yd, (k, 0), up)
        copies["y1", k] = send(out.at[k, behind], rec.at[k, y], yd, (k, 1), down)
        rec[k, y] = out[k, y]

    def pass_on(k):
        ahead, behind = lax.rem(y + 1, 4), lax.rem(y + 3, 4)
        first, second = pl.ds(0, 2 * cap), pl.ds(2 * cap, 2 * cap)
        copies["f0", k].wait_recv()
        copies["g0", k] = send(fr.at[k], rec.at[k, behind, first], yg, (k, 0), up)
        copies["f1", k].wait_recv()
        copies["g1", k] = send(fl.at[k], rec.at[k, ahead, second], yg, (k, 1), down)

    def gram(k):
        for name in ("y0", "y1", "g0", "g1"):
            copies[name, k].wait_recv()

        done = []
        for d in (2, 1, 3, 0):
            to = lax.rem(x + d, 4)
            lines = pl.ds(pl.multiple_of(to * cap, cap), cap)
            got = jnp.concatenate([rec[k, i, lines, :] for i in range(4)])
            fit = jnp.dot(
                bsel[to], c2[:, k * crows : (k + 1) * crows], preferred_element_type=F32
            )
            got = (got.astype(F32) - fit).astype(BF16)
            hits = jnp.dot(place[to], got, preferred_element_type=F32).astype(BF16)
            for p in range(4):
                h = hits[p * 128 : (p + 1) * 128]
                g = lax.dot_general(h, h, NT, preferred_element_type=F32)
                if k > 0:
                    g = gacc[to, p] + g
                if k == CHUNKS - 1 and d > 0:
                    gsend[d - 1, p] = g.astype(BF16)
                else:
                    gacc[to, p] = g
            if k == CHUNKS - 1 and d > 0:
                done.append(send(gsend.at[d - 1], grecv.at[d - 1], gr, d - 1, at_x(d)))
        return done

    gather_own(0)
    gather_own(1)

    ours = pl.multiple_of(core * wide, wide)
    cf[0:n_cov, :] = cov[...]
    cf[n_cov:, :] = jnp.zeros((CP - n_cov, rows), F32)
    cv = cf[...]
    c_1 = cv.astype(BF16)
    c_2 = (cv - c_1.astype(F32)).astype(BF16)
    c_3 = (cv - c_1.astype(F32) - c_2.astype(F32)).astype(BF16)
    c3v = jnp.concatenate([c_1, c_2, c_3])
    gap = jnp.zeros((CB - CP, rows), F32)
    stacked = jnp.concatenate([c_1.astype(F32), gap, c_2.astype(F32), gap])
    c2[...] = stacked.astype(BF16)
    ct[...] = stacked.T.astype(BF16)
    cd = jnp.dot(c3v, dos[:, pl.ds(ours, wide)], preferred_element_type=F32)
    cq = jnp.dot(c3v, prot[...], preferred_element_type=F32)
    cc = lax.dot_general(cv, cv, NT, precision=BEST, preferred_element_type=F32)
    arb[x, :, 0:wide] = cd[0:CP] + cd[CP : 2 * CP] + cd[2 * CP :]
    arb[x, :, wide : wide + n_prot] = cq[0:CP] + cq[CP : 2 * CP] + cq[2 * CP :]
    arb[x, :, wide + n_prot :] = jnp.zeros((CP, 128), F32)
    arb[x, :, wide + n_prot : wide + n_prot + CP] = cc
    sums = [send(arb.at[x], arb.at[x], ar, d - 1, at_x(d)) for d in (1, 2, 3)]

    flat = 4 * slots
    lane = lax.broadcasted_iota(jnp.int32, (1, slots), 1)
    lists, lives = [], []
    for yy in range(4):
        for s in range(4):
            g = s * 16 + zl * 4 + yy
            lists.append(jnp.concatenate([hidx[g, p : p + 1, :] for p in range(4)], axis=1))
            lives.append(
                jnp.concatenate([lane < hcnt[g, p : p + 1, :] for p in range(4)], axis=1)
            )
    lists = jnp.concatenate(lists).astype(F32)
    lives = jnp.concatenate([jnp.where(one, 1.0, 0.0) for one in lives])
    block = jnp.floor(lists * (1.0 / v_dev))
    far = jnp.floor(block * 0.25)
    line = block - 4.0 * far
    upper = jnp.where(
        lax.broadcasted_iota(jnp.int32, (flat, flat), 0)
        <= lax.broadcasted_iota(jnp.int32, (flat, flat), 1),
        1.0,
        0.0,
    ).astype(BF16)
    chosen = jnp.where(line == y.astype(F32), lives, 0.0)
    rank = jnp.dot(chosen.astype(BF16), upper, preferred_element_type=F32)
    ranks[...] = jnp.where(chosen > 0.0, rank, 0.0)
    slot = zl.astype(F32) - far
    slot = jnp.where(slot < 0.0, slot + 4.0, slot)
    places[...] = lists + (slot - block) * v_dev + 1.0
    pos_of = jnp.where(lives > 0.0, line * cap, -1.0)
    for i in range(4):
        member = jnp.where(line == i, lives, 0.0)
        rank = jnp.dot(member.astype(BF16), upper, preferred_element_type=F32)
        pos_of = pos_of + jnp.where(member > 0.0, rank - 1.0, 0.0)
    slot_pos[...] = pos_of

    def column(t, carry):
        order = lax.broadcasted_iota(jnp.int32, (cap, flat), 0).astype(F32) + 1.0
        found = jnp.where(ranks[pl.ds(t, 1), :] == order, places[pl.ds(t, 1), :], 0.0)
        found = jnp.sum(found, axis=1, keepdims=True) - 1.0
        high = jnp.floor(found * (1.0 / 256.0))
        lows[t] = jnp.broadcast_to(found - 256.0 * high, (cap, 128)).astype(BF16)
        highs[t] = jnp.broadcast_to(high, (cap, 128)).astype(BF16)
        return carry

    lax.fori_loop(0, 16, column, 0)

    near = lax.broadcasted_iota(jnp.int32, (cap, 128), 1).astype(F32)
    near = (near.astype(BF16), (near + 128.0).astype(BF16))
    one_b, zero_b = jnp.ones((cap, 128), BF16), jnp.zeros((cap, 128), BF16)

    def build(t, carry):
        lines = pl.ds(pl.multiple_of(lax.rem(t, 4) * cap, cap), cap)
        low_of, high_of = lows[t], highs[t]
        for part in range(4 * v_dev // 256):
            here = jnp.where(high_of == jnp.full((cap, 128), part, BF16), low_of, -one_b)
            for i in range(2):
                at = part * 256 + i * 128
                pick[t // 4, lines, at : at + 128] = jnp.where(here == near[i], one_b, zero_b)
        return carry

    lax.fori_loop(0, 8, build, 0)
    gather_on(0)
    gather_own(2)
    lax.fori_loop(8, 16, build, 0)
    gather_on(1)
    gather_own(3)
    gather_far(0)
    choose(0)

    def put(s, carry):
        want = jnp.broadcast_to(slot_pos[pl.ds(y * 4 + s, 1), :], (128, flat)).T
        here = lax.broadcasted_iota(jnp.int32, (flat, 128), 1).astype(F32)
        for i in range(4 * cap // 128):
            place[s, :, i * 128 : (i + 1) * 128] = jnp.where(
                want == here + float(i * 128), 1.0, 0.0
            ).astype(BF16)
        return carry

    lax.fori_loop(0, 4, put, 0)

    gather_far(1)
    choose(1)

    for copy in sums:
        copy.wait_recv()
    total = arb[0] + arb[1] + arb[2] + arb[3]
    lane = lax.broadcasted_iota(jnp.int32, (CP, 128), 1)
    row = lax.broadcasted_iota(jnp.int32, (CP, 128), 0)
    both = total[:, wide + n_prot :]
    both = both + jnp.where((lane == row) & (row >= n_cov), 1.0, 0.0)
    both = both + jnp.where(lane == row + 64, 1.0, 0.0)
    unit = lax.broadcasted_iota(jnp.int32, (CP, 1), 0)
    for i in range(n_cov):
        scaled = both[i : i + 1, :] / both[i : i + 1, i : i + 1]
        both = both - (both[:, i : i + 1] - jnp.where(unit == i, 1.0, 0.0)) * scaled
    inverse = pltpu.roll(both, 64, 1)[:, 0:CP]
    coef = jnp.dot(
        inverse, total[:, : wide + n_prot], precision=BEST, preferred_element_type=F32
    )

    bt[0, core, 0:CP, :] = coef[:, :wide].astype(BF16)
    bt[0, core, CP:CB, :] = jnp.zeros((CB - CP, wide), BF16)
    low, high = pl.ds(0, CB // 2), pl.ds(CB // 2, CB // 2)
    b_a = send(bt.at[0, core], bt.at[1, core], bag, 0, right)
    b_b = send(bt.at[0, core], bt.at[3, core], bag, 1, left)
    b_s = [send(bt.at[0, core], bt.at[0, core], bsw, 0, sibling)]

    gather_on(2)
    pass_on(0)
    gather_far(2)
    choose(2)
    gather_on(3)
    pass_on(1)

    cb = coef[:, wide:]
    ch = cb.astype(BF16)
    cm = (cb - ch.astype(F32)).astype(BF16)
    gap = jnp.zeros((CB - CP, n_prot), BF16)
    ctv = ct[...]
    fit = jnp.dot(ctv, jnp.concatenate([ch, gap, ch, gap]), preferred_element_type=F32)
    fit = fit + jnp.dot(ctv, jnp.concatenate([cm, gap, cm, gap]), preferred_element_type=F32)
    res = (prot[...].astype(F32) - fit).astype(BF16).astype(F32)
    auxb[x, :, v_dev:] = jnp.broadcast_to(
        jnp.sum(res * res, axis=0, keepdims=True), (8, n_prot)
    )
    prt[...] = res.T.astype(BF16)

    b_a.wait_recv()
    b_c = send(bt.at[1, core, high], bt.at[2, core, high], bfw, 0, right)
    b_s.append(send(bt.at[1, core], bt.at[1, core], bsw, 1, sibling))
    b_b.wait_recv()
    b_d = send(bt.at[3, core, low], bt.at[2, core, low], bfw, 1, left)
    b_s.append(send(bt.at[3, core], bt.at[3, core], bsw, 2, sibling))

    b_s[0].wait_recv()
    for side in range(2):
        part = bt[0, side]
        bc[0:CB, side * wide : (side + 1) * wide] = part
        bc[CB:, side * wide : (side + 1) * wide] = part


    def own_residual(k, squares):
        here = pl.ds(pl.multiple_of(k * crows, crows), crows)
        fit = jnp.dot(ct[here, :], bc[...], preferred_element_type=F32)
        res = dos[here, :].astype(F32) - fit
        d2own[here, :] = res.astype(BF16)
        return squares + jnp.sum(res * res, axis=0, keepdims=True)

    squares = lax.fori_loop(0, CHUNKS, own_residual, jnp.zeros((1, v_dev), F32))
    auxb[x, :, :v_dev] = jnp.broadcast_to(squares, (8, v_dev))
    own = v_dev // 4

    def score(i, carry):
        cols = pl.ds(pl.multiple_of(i * own, own), own)
        ssend[i] = jnp.dot(prt[...], d2own[:, cols], preferred_element_type=F32).astype(BF16)
        return carry

    lax.fori_loop(0, 4, score, 0)
    s_c = [
        send(ssend.at[lax.rem(x + d, 4)], srecv.at[d - 1], sc, d - 1, at_x(d)) for d in (1, 2, 3)
    ]
    a_c = [send(auxb.at[x], auxb.at[x], ax, d - 1, at_x(d)) for d in (1, 2, 3)]

    gather_far(3)
    choose(3)
    pass_on(2)

    b_c.wait_recv()
    b_d.wait_recv()
    b_s.append(send(bt.at[2, core], bt.at[2, core], bsw, 3, sibling))
    for copy in b_s[1:]:
        copy.wait_recv()

    def coefs(to, carry):
        part = jnp.zeros((CB, 4 * cap), F32)
        for slot in range(4):
            for side in range(2):
                at = slot * v_dev + side * wide
                part = part + lax.dot_general(
                    bt[slot, side], pick[to, :, at : at + wide], NT, preferred_element_type=F32
                )
        bout[to] = part.astype(BF16)
        return carry

    lax.fori_loop(0, 4, coefs, 0)
    ahead, behind, across = lax.rem(y + 1, 4), lax.rem(y + 3, 4), lax.rem(y + 2, 4)
    h_f = [
        send(bout.at[across, low], bfr, hf, 0, up),
        send(bout.at[across, high], bfl, hf, 1, down),
    ]
    h_c = [
        send(bout.at[ahead], brec.at[y], hd, 0, up),
        send(bout.at[behind], brec.at[y], hd, 1, down),
    ]
    brec[y] = bout[y]

    h_f[0].wait_recv()
    h_c.append(send(bfr, brec.at[behind, low], hg, 0, up))
    h_f[1].wait_recv()
    h_c.append(send(bfl, brec.at[ahead, high], hg, 1, down))
    for copy in h_c:
        copy.wait_recv()
    for to in range(4):
        for i in range(4):
            part = brec[i, :, to * cap : (to + 1) * cap].astype(F32)
            part = jnp.concatenate([part, part]).T.astype(BF16)
            bsel[to, i * cap : (i + 1) * cap, :] = part
    gram(0)
    pass_on(3)
    for copy in s_c + a_c:
        copy.wait_recv()
    auxs[...] = auxb[0] + auxb[1] + auxb[2] + auxb[3]
    quarter_v = pl.ds(pl.multiple_of(x * own, own), own)
    dos_var = auxs[0:1, quarter_v]
    rss = auxs[0:1, v_dev:]
    whole = ssend[x].astype(F32)
    for d in range(3):
        whole = whole + srecv[d].astype(F32)
    whole = (whole / jnp.sqrt(dos_var)).T / jnp.sqrt(rss / freedom + 1e-05)
    zbuf[quarter_v, :] = whole.astype(BF16)
    z_c = [send(zbuf.at[quarter_v], zbuf.at[quarter_v], zg, d - 1, at_x(d)) for d in (1, 2, 3)]
    gram(1)
    gram(2)
    for copy in z_c:
        copy.wait_recv()
    z_out[...] = zbuf[...]
    g_c = gram(3)
    whole = gacc[x]
    for copy in g_c:
        copy.wait_recv()
    for d in range(3):
        whole = whole + grecv[d].astype(F32)
    g_out[...] = whole
    for copy in sent:
        copy.wait_send()


def shards(n_z, dosages, proteins, covariates, hit_index, hit_count):
    n_sample = lax.axis_size("sample")
    n_variant = lax.axis_size("variant")
    rows, v_dev = dosages.shape
    n_prot = proteins.shape[1]
    n_cov = covariates.shape[0]
    samples = rows * n_sample
    n_dest, p_own, slots = hit_index.shape
    flat = p_own * slots
    block_hits = max(p_own * 16, 2 * slots)
    most = 3 * block_hits // n_variant
    other = -(-(block_hits - most) // (n_variant - 1))
    cap = -(-(most + 3 * other) // 16) * 16
    def vmem(shape, dtype=BF16):
        return pltpu.VMEM(shape, dtype)

    def pair(shape):
        return [pltpu.SemaphoreType.DMA(shape)] * 2

    crows = rows // CHUNKS
    own = v_dev // 4
    scratch = [
        vmem((3, rows, v_dev)),
        vmem((rows, v_dev)),
        vmem((4, 4 * cap, 4 * v_dev)),
        vmem((CHUNKS, 4, 4 * cap, crows)),
        vmem((CHUNKS, 4, 4 * cap, crows)),
        vmem((CHUNKS, 2 * cap, crows)),
        vmem((CHUNKS, 2 * cap, crows)),
        vmem((4, CP, v_dev // 2 + n_prot + 128), F32),
        vmem((4, 2, CB, v_dev // 2)),
        vmem((2 * CB, v_dev)),
        vmem((n_prot, rows)),
        vmem((4, n_prot, own)),
        vmem((3, n_prot, own)),
        vmem((4, 8, v_dev + n_prot), F32),
        vmem((8, v_dev + n_prot), F32),
        vmem((v_dev, n_prot)),
        vmem((4, p_own, slots, slots), F32),
        vmem((3, p_own, slots, slots)),
        vmem((3, p_own, slots, slots)),
        vmem((CP, rows), F32),
        vmem((rows, 2 * CB)),
        vmem((2 * CB, rows)),
        vmem((16, flat), F32),
        vmem((16, flat), F32),
        vmem((16, flat), F32),
        vmem((16, cap, 128)),
        vmem((16, cap, 128)),
        vmem((4, flat, 4 * cap)),
        vmem((4, CB, 4 * cap)),
        vmem((4, CB, 4 * cap)),
        vmem((CB // 2, 4 * cap)),
        vmem((CB // 2, 4 * cap)),
        vmem((4, 4 * cap, 2 * CB)),
        *pair((CHUNKS, 2)),
        *pair((CHUNKS, 2)),
        *pair((CHUNKS, 3)),
        *pair((2,)),
        *pair((2,)),
        *pair((4,)),
        *pair((3,)),
        *pair((3,)),
        *pair((3,)),
        *pair((3,)),
        *pair((3,)),
        *pair((CHUNKS, 2)),
        *pair((CHUNKS, 2)),
        *pair((CHUNKS, 2)),
        *pair((2,)),
        *pair((2,)),
        *pair((2,)),
    ]
    z, g = pl.pallas_call(
        functools.partial(kernel, n_z, n_cov, cap, float(samples - n_cov)),
        out_shape=(
            jax.ShapeDtypeStruct((v_dev, n_prot), BF16),
            jax.ShapeDtypeStruct((p_own, slots, slots), F32),
        ),
        in_specs=[pl.BlockSpec(memory_space=pltpu.VMEM)] * 5,
        out_specs=(pl.BlockSpec(memory_space=pltpu.VMEM),) * 2,
        scratch_shapes=scratch,
        compiler_params=pltpu.CompilerParams(
            collective_id=0, has_side_effects=True, vmem_limit_bytes=58 * 1024 * 1024
        ),
    )(dosages, proteins, covariates, hit_index, hit_count[:, :, None])
    return (z.astype(F32), g / F32(samples))


def solution(mesh):
    in_specs = (
        P("sample", "variant"),
        P("sample", "protein"),
        P(None, "sample"),
        P(None, "protein", None),
        P(None, "protein"),
    )
    out_specs = (P("variant", "protein"), P(("sample", "variant", "protein"), None, None))
    n_z = 4 * (mesh.shape["protein"] // 2)
    return jax.shard_map(
        functools.partial(shards, n_z),
        mesh=mesh,
        in_specs=in_specs,
        out_specs=out_specs,
        check_vma=False,
    )
```

time: 123 us -> 114 us (0.927)
  local copies, waits for them, and re-layouts: 6.87 us -> 1.45 us
  other arithmetic: 7.44 us -> 3.76 us
    reshape x3 -> x0, local copies, waits for them, and re-layouts: 3.33 us -> none  [the longest x1 1.57 us: shards(): col = jnp.sum(jnp.where(rank[:, :, None, :] == places[:, None], column[:,...]
    select_n x2 -> x0, other arithmetic: 1.53 us -> none  [the longest x1 1.52 us: shards(): jnp.where(own_live, own_line * cap + rank_in, -1).reshape(n_sample, flat, 1)]
    broadcast_in_dim x1, local copies, waits for them, and re-layouts: 0.04 us -> 1.45 us  [shards(): hit_count[:, :, None]]
where the time goes in v3:
time: 114 us
  Pallas kernels  108 us (95%)
  other arithmetic  3.76 us (3%)
  local copies, waits for them, and re-layouts  1.45 us (1%)
    pallas_call x1, Pallas kernels, shards(): pl.pallas_call(functools.partial(kernel, n_z, n_cov, cap, float(samples -...  108 us

profile of v3, /device:TPU:1, one launch (start us, length us, event | category | flops | bytes accessed | tf_op | source)
XLA Modules:
  0.0 114.2 jit_solution(16170363372248824984)
XLA Ops:
  0.6 1.5 %copy.8.hcnt = s32[64,4,1]{2,1,0:T(4,128)} copy(s32[64,4,1]{0,1,2:T(4,128)} %bitcast.1) | data formatting | bytes 2048 | tf_op jit(solution)/shard_map/broadcast_in_dim | solution.py:509
  2.1 108.3 %shard_map.68 = (bf16[1024,256]{1,0:T(8,128)(2,1)}, f32[4,128,128]{2,1,0:T(8,128)}) custom-call(bf16[1024,1024]{1,0:T(8,128)(2,1)} %dos.1, bf16[1024,256]{1,0:T(8,128)(2,1)} %prot.1, f32[44,1024]{1,0:T(8,128)} %cov.1, s32[64,4,128]{2,1,0:T(4,128)} %hidx.1, s32[64,4,1]{2,1,0:T(4,128)} %copy.8.hcnt), custom_call_target="tpu_custom_call" | custom-call | tf_op jit(solution)/shard_map/pallas_call | solution.py:497
  110.4 1.7 %broadcast_multiply_fusion = f32[4,128,128]{2,1,0:T(8,128)} fusion(f32[4,128,128]{2,1,0:T(8,128)} %get-tuple-element.5), kind=kLoop, calls=%fused_computation | loop fusion | flops 65536 | bytes 524288 | tf_op jit(solution)/shard_map/div | solution.py:510
  112.1 2.1 %convert_element_type.3 = f32[1024,256]{1,0:T(8,128)} convert(bf16[1024,256]{1,0:T(8,128)(2,1)} %get-tuple-element.4) | non-fusion elementwise | flops 262144 | bytes 1572864 | tf_op jit(solution)/shard_map/convert_element_type | solution.py:510

commit v4 on v3

--- a/solution.py
+++ b/solution.py
@@ -103,7 +103,8 @@
         for slot in range(3):
             copies["s%d" % slot, k].wait_recv()
 
-        def one(to, carry):
+        def one(d, carry):
+            to = lax.rem(y + d, 4)
             part = lax.dot_general(
                 pick[to, :, 0:v_dev], dos[here, :], NT, preferred_element_type=F32
             )
@@ -117,11 +118,12 @@
             out[k, to] = part.astype(BF16)
             return carry
 
-        lax.fori_loop(0, 4, one, 0)
         ahead, behind, across = lax.rem(y + 1, 4), lax.rem(y + 3, 4), lax.rem(y + 2, 4)
         first, second = pl.ds(0, 2 * cap), pl.ds(2 * cap, 2 * cap)
+        one(2, 0)
         copies["f0", k] = send(out.at[k, across, first], fr.at[k], yf, (k, 0), up)
         copies["f1", k] = send(out.at[k, across, second], fl.at[k], yf, (k, 1), down)
+        lax.fori_loop(3, 6, one, 0)
         copies["y0", k] = send(out.at[k, ahead], rec.at[k, y], yd, (k, 0), up)
         copies["y1", k] = send(out.at[k, behind], rec.at[k, y], yd, (k, 1), down)
         rec[k, y] = out[k, y]
@@ -163,27 +165,6 @@
 
     gather_own(0)
     gather_own(1)
-
-    ours = pl.multiple_of(core * wide, wide)
-    cf[0:n_cov, :] = cov[...]
-    cf[n_cov:, :] = jnp.zeros((CP - n_cov, rows), F32)
-    cv = cf[...]
-    c_1 = cv.astype(BF16)
-    c_2 = (cv - c_1.astype(F32)).astype(BF16)
-    c_3 = (cv - c_1.astype(F32) - c_2.astype(F32)).astype(BF16)
-    c3v = jnp.concatenate([c_1, c_2, c_3])
-    gap = jnp.zeros((CB - CP, rows), F32)
-    stacked = jnp.concatenate([c_1.astype(F32), gap, c_2.astype(F32), gap])
-    c2[...] = stacked.astype(BF16)
-    ct[...] = stacked.T.astype(BF16)
-    cd = jnp.dot(c3v, dos[:, pl.ds(ours, wide)], preferred_element_type=F32)
-    cq = jnp.dot(c3v, prot[...], preferred_element_type=F32)
-    cc = lax.dot_general(cv, cv, NT, precision=BEST, preferred_element_type=F32)
-    arb[x, :, 0:wide] = cd[0:CP] + cd[CP : 2 * CP] + cd[2 * CP :]
-    arb[x, :, wide : wide + n_prot] = cq[0:CP] + cq[CP : 2 * CP] + cq[2 * CP :]
-    arb[x, :, wide + n_prot :] = jnp.zeros((CP, 128), F32)
-    arb[x, :, wide + n_prot : wide + n_prot + CP] = cc
-    sums = [send(arb.at[x], arb.at[x], ar, d - 1, at_x(d)) for d in (1, 2, 3)]
 
     flat = 4 * slots
     lane = lax.broadcasted_iota(jnp.int32, (1, slots), 1)
@@ -244,10 +225,31 @@
                 pick[t // 4, lines, at : at + 128] = jnp.where(here == near[i], one_b, zero_b)
         return carry
 
-    lax.fori_loop(0, 8, build, 0)
+    lax.fori_loop(0, 16, build, 0)
     gather_on(0)
     gather_own(2)
-    lax.fori_loop(8, 16, build, 0)
+
+    ours = pl.multiple_of(core * wide, wide)
+    cf[0:n_cov, :] = cov[...]
+    cf[n_cov:, :] = jnp.zeros((CP - n_cov, rows), F32)
+    cv = cf[...]
+    c_1 = cv.astype(BF16)
+    c_2 = (cv - c_1.astype(F32)).astype(BF16)
+    c_3 = (cv - c_1.astype(F32) - c_2.astype(F32)).astype(BF16)
+    c3v = jnp.concatenate([c_1, c_2, c_3])
+    gap = jnp.zeros((CB - CP, rows), F32)
+    stacked = jnp.concatenate([c_1.astype(F32), gap, c_2.astype(F32), gap])
+    c2[...] = stacked.astype(BF16)
+    ct[...] = stacked.T.astype(BF16)
+    cd = jnp.dot(c3v, dos[:, pl.ds(ours, wide)], preferred_element_type=F32)
+    cq = jnp.dot(c3v, prot[...], preferred_element_type=F32)
+    cc = lax.dot_general(cv, cv, NT, precision=BEST, preferred_element_type=F32)
+    arb[x, :, 0:wide] = cd[0:CP] + cd[CP : 2 * CP] + cd[2 * CP :]
+    arb[x, :, wide : wide + n_prot] = cq[0:CP] + cq[CP : 2 * CP] + cq[2 * CP :]
+    arb[x, :, wide + n_prot :] = jnp.zeros((CP, 128), F32)
+    arb[x, :, wide + n_prot : wide + n_prot + CP] = cc
+    sums = [send(arb.at[x], arb.at[x], ar, d - 1, at_x(d)) for d in (1, 2, 3)]
+
     gather_on(1)
     gather_own(3)
     gather_far(0)
@@ -265,7 +267,10 @@
     lax.fori_loop(0, 4, put, 0)
 
     gather_far(1)
+    gather_on(2)
     choose(1)
+    gather_on(3)
+    pass_on(0)
 
     for copy in sums:
         copy.wait_recv()
@@ -291,11 +296,17 @@
     b_b = send(bt.at[0, core], bt.at[3, core], bag, 1, left)
     b_s = [send(bt.at[0, core], bt.at[0, core], bsw, 0, sibling)]
 
-    gather_on(2)
-    pass_on(0)
     gather_far(2)
     choose(2)
-    gather_on(3)
+    b_a.wait_recv()
+    b_c = send(bt.at[1, core, high], bt.at[2, core, high], bfw, 0, right)
+    b_s.append(send(bt.at[1, core], bt.at[1, core], bsw, 1, sibling))
+    b_b.wait_recv()
+    b_d = send(bt.at[3, core, low], bt.at[2, core, low], bfw, 1, left)
+    b_s.append(send(bt.at[3, core], bt.at[3, core], bsw, 2, sibling))
+
+    b_s[0].wait_recv()
+    gather_far(3)
     pass_on(1)
 
     cb = coef[:, wide:]
@@ -311,14 +322,6 @@
     )
     prt[...] = res.T.astype(BF16)
 
-    b_a.wait_recv()
-    b_c = send(bt.at[1, core, high], bt.at[2, core, high], bfw, 0, right)
-    b_s.append(send(bt.at[1, core], bt.at[1, core], bsw, 1, sibling))
-    b_b.wait_recv()
-    b_d = send(bt.at[3, core, low], bt.at[2, core, low], bfw, 1, left)
-    b_s.append(send(bt.at[3, core], bt.at[3, core], bsw, 2, sibling))
-
-    b_s[0].wait_recv()
     for side in range(2):
         part = bt[0, side]
         bc[0:CB, side * wide : (side + 1) * wide] = part
@@ -346,10 +349,6 @@
         send(ssend.at[lax.rem(x + d, 4)], srecv.at[d - 1], sc, d - 1, at_x(d)) for d in (1, 2, 3)
     ]
     a_c = [send(auxb.at[x], auxb.at[x], ax, d - 1, at_x(d)) for d in (1, 2, 3)]
-
-    gather_far(3)
-    choose(3)
-    pass_on(2)
 
     b_c.wait_recv()
     b_d.wait_recv()
@@ -380,6 +379,8 @@
     ]
     brec[y] = bout[y]
 
+    choose(3)
+    pass_on(2)
     h_f[0].wait_recv()
     h_c.append(send(bfr, brec.at[behind, low], hg, 0, up))
     h_f[1].wait_recv()
@@ -392,6 +393,7 @@
             part = jnp.concatenate([part, part]).T.astype(BF16)
             bsel[to, i * cap : (i + 1) * cap, :] = part
     gram(0)
+    gram(1)
     pass_on(3)
     for copy in s_c + a_c:
         copy.wait_recv()
@@ -405,7 +407,6 @@
     whole = (whole / jnp.sqrt(dos_var)).T / jnp.sqrt(rss / freedom + 1e-05)
     zbuf[quarter_v, :] = whole.astype(BF16)
     z_c = [send(zbuf.at[quarter_v], zbuf.at[quarter_v], zg, d - 1, at_x(d)) for d in (1, 2, 3)]
-    gram(1)
     gram(2)
     for copy in z_c:
         copy.wait_recv()

time: 114 us -> 110 us (0.965)
  Pallas kernels: 108 us -> 104 us
    pallas_call x1, Pallas kernels: 108 us -> 104 us  [shards(): pl.pallas_call(functools.partial(kernel, n_z, n_cov, cap, float(samples -...]
where the time goes in v4:
time: 110 us; the launch traced here: 109 us
  Pallas kernels  104 us (95%)
  other arithmetic  3.76 us (3%)
  local copies, waits for them, and re-layouts  1.45 us (1%)
    pallas_call x1, Pallas kernels, shards(): pl.pallas_call(functools.partial(kernel, n_z, n_cov, cap, float(samples -...  104 us

profile of v4, /device:TPU:1, one launch (start us, length us, event | category | flops | bytes accessed | tf_op | source)
XLA Modules:
  0.0 109.4 jit_solution(6780608229385352400)
XLA Ops:
  0.6 1.5 %copy.8.hcnt = s32[64,4,1]{2,1,0:T(4,128)} copy(s32[64,4,1]{0,1,2:T(4,128)} %bitcast.1) | data formatting | bytes 2048 | tf_op jit(solution)/shard_map/broadcast_in_dim | solution.py:510
  2.1 103.5 %shard_map.68 = (bf16[1024,256]{1,0:T(8,128)(2,1)}, f32[4,128,128]{2,1,0:T(8,128)}) custom-call(bf16[1024,1024]{1,0:T(8,128)(2,1)} %dos.1, bf16[1024,256]{1,0:T(8,128)(2,1)} %prot.1, f32[44,1024]{1,0:T(8,128)} %cov.1, s32[64,4,128]{2,1,0:T(4,128)} %hidx.1, s32[64,4,1]{2,1,0:T(4,128)} %copy.8.hcnt), custom_call_target="tpu_custom_call" | custom-call | tf_op jit(solution)/shard_map/pallas_call | solution.py:498
  105.6 1.7 %broadcast_multiply_fusion = f32[4,128,128]{2,1,0:T(8,128)} fusion(f32[4,128,128]{2,1,0:T(8,128)} %get-tuple-element.5), kind=kLoop, calls=%fused_computation | loop fusion | flops 65536 | bytes 524288 | tf_op jit(solution)/shard_map/div | solution.py:511
  107.3 2.1 %convert_element_type.3 = f32[1024,256]{1,0:T(8,128)} convert(bf16[1024,256]{1,0:T(8,128)(2,1)} %get-tuple-element.4) | non-fusion elementwise | flops 262144 | bytes 1572864 | tf_op jit(solution)/shard_map/convert_element_type | solution.py:511

commit v5 on v4

--- a/solution.py
+++ b/solution.py
@@ -19,11 +19,11 @@
 
 def kernel(n_z, n_cov, cap, freedom, dos, prot, cov, hidx, hcnt, z_out, g_out, *scratch):
     (
-        dall, d2own, pick, out, rec, fr, fl, arb, bt, bc, prt, ssend, srecv, auxb, auxs, zbuf,
+        dall, d2own, pick, out, rec, arb, bt, bc, prt, ssend, srecv, auxb, auxs, zbuf,
         gacc, gsend, grecv, cf, ct, c2, ranks, places, slot_pos, lows, highs, place,
-        bout, brec, bfr, bfl, bsel, *sems,
+        bout, brec, bsel, *sems,
     ) = scratch
-    ag, fw, sw, bag, bfw, bsw, ar, sc, ax, zg, gr, yd, yf, yg, hd, hf, hg = zip(sems[0::2], sems[1::2])
+    ag, fw, sw, bag, bfw, bsw, ar, sc, ax, zg, gr, yd, hd = zip(sems[0::2], sems[1::2])
 
     x = lax.axis_index("sample")
     v = lax.axis_index("variant")
@@ -43,9 +43,9 @@
         return (x, lax.rem(there, 4) * 4 + y, (there // 4) * 2 + core)
 
     right, left, sibling = at_z(1), at_z(-1), (x, v, zh * 2 + 1 - core)
-    up, down = at_y(1), at_y(3)
-
-    neighbours = [at_x(1), at_x(2), at_x(3), up, down, right, left, sibling]
+    up, down, opposite = at_y(1), at_y(3), at_y(2)
+
+    neighbours = [at_x(1), at_x(2), at_x(3), up, down, opposite, right, left, sibling]
     barrier = pltpu.get_barrier_semaphore()
     for there in neighbours:
         pl.semaphore_signal(barrier, inc=1, device_id=there, device_id_type=MESH)
@@ -119,25 +119,15 @@
             return carry
 
         ahead, behind, across = lax.rem(y + 1, 4), lax.rem(y + 3, 4), lax.rem(y + 2, 4)
-        first, second = pl.ds(0, 2 * cap), pl.ds(2 * cap, 2 * cap)
         one(2, 0)
-        copies["f0", k] = send(out.at[k, across, first], fr.at[k], yf, (k, 0), up)
-        copies["f1", k] = send(out.at[k, across, second], fl.at[k], yf, (k, 1), down)
+        copies["y2", k] = send(out.at[k, across], rec.at[k, y], yd, (k, 2), opposite)
         lax.fori_loop(3, 6, one, 0)
         copies["y0", k] = send(out.at[k, ahead], rec.at[k, y], yd, (k, 0), up)
         copies["y1", k] = send(out.at[k, behind], rec.at[k, y], yd, (k, 1), down)
         rec[k, y] = out[k, y]
 
-    def pass_on(k):
-        ahead, behind = lax.rem(y + 1, 4), lax.rem(y + 3, 4)
-        first, second = pl.ds(0, 2 * cap), pl.ds(2 * cap, 2 * cap)
-        copies["f0", k].wait_recv()
-        copies["g0", k] = send(fr.at[k], rec.at[k, behind, first], yg, (k, 0), up)
-        copies["f1", k].wait_recv()
-        copies["g1", k] = send(fl.at[k], rec.at[k, ahead, second], yg, (k, 1), down)
-
     def gram(k):
-        for name in ("y0", "y1", "g0", "g1"):
+        for name in ("y0", "y1", "y2"):
             copies[name, k].wait_recv()
 
         done = []
@@ -270,7 +260,6 @@
     gather_on(2)
     choose(1)
     gather_on(3)
-    pass_on(0)
 
     for copy in sums:
         copy.wait_recv()
@@ -307,7 +296,6 @@
 
     b_s[0].wait_recv()
     gather_far(3)
-    pass_on(1)
 
     cb = coef[:, wide:]
     ch = cb.astype(BF16)
@@ -369,32 +357,15 @@
 
     lax.fori_loop(0, 4, coefs, 0)
     ahead, behind, across = lax.rem(y + 1, 4), lax.rem(y + 3, 4), lax.rem(y + 2, 4)
-    h_f = [
-        send(bout.at[across, low], bfr, hf, 0, up),
-        send(bout.at[across, high], bfl, hf, 1, down),
-    ]
     h_c = [
+        send(bout.at[across], brec.at[y], hd, 2, opposite),
         send(bout.at[ahead], brec.at[y], hd, 0, up),
         send(bout.at[behind], brec.at[y], hd, 1, down),
     ]
     brec[y] = bout[y]
 
     choose(3)
-    pass_on(2)
-    h_f[0].wait_recv()
-    h_c.append(send(bfr, brec.at[behind, low], hg, 0, up))
-    h_f[1].wait_recv()
-    h_c.append(send(bfl, brec.at[ahead, high], hg, 1, down))
-    for copy in h_c:
-        copy.wait_recv()
-    for to in range(4):
-        for i in range(4):
-            part = brec[i, :, to * cap : (to + 1) * cap].astype(F32)
-            part = jnp.concatenate([part, part]).T.astype(BF16)
-            bsel[to, i * cap : (i + 1) * cap, :] = part
-    gram(0)
-    gram(1)
-    pass_on(3)
+
     for copy in s_c + a_c:
         copy.wait_recv()
     auxs[...] = auxb[0] + auxb[1] + auxb[2] + auxb[3]
@@ -407,11 +378,21 @@
     whole = (whole / jnp.sqrt(dos_var)).T / jnp.sqrt(rss / freedom + 1e-05)
     zbuf[quarter_v, :] = whole.astype(BF16)
     z_c = [send(zbuf.at[quarter_v], zbuf.at[quarter_v], zg, d - 1, at_x(d)) for d in (1, 2, 3)]
+
+    for copy in h_c:
+        copy.wait_recv()
+    for to in range(4):
+        for i in range(4):
+            part = brec[i, :, to * cap : (to + 1) * cap].astype(F32)
+            part = jnp.concatenate([part, part]).T.astype(BF16)
+            bsel[to, i * cap : (i + 1) * cap, :] = part
+    gram(0)
+    gram(1)
     gram(2)
+    g_c = gram(3)
     for copy in z_c:
         copy.wait_recv()
     z_out[...] = zbuf[...]
-    g_c = gram(3)
     whole = gacc[x]
     for copy in g_c:
         copy.wait_recv()
@@ -449,8 +430,6 @@
         vmem((4, 4 * cap, 4 * v_dev)),
         vmem((CHUNKS, 4, 4 * cap, crows)),
         vmem((CHUNKS, 4, 4 * cap, crows)),
-        vmem((CHUNKS, 2 * cap, crows)),
-        vmem((CHUNKS, 2 * cap, crows)),
         vmem((4, CP, v_dev // 2 + n_prot + 128), F32),
         vmem((4, 2, CB, v_dev // 2)),
         vmem((2 * CB, v_dev)),
@@ -474,8 +453,6 @@
         vmem((4, flat, 4 * cap)),
         vmem((4, CB, 4 * cap)),
         vmem((4, CB, 4 * cap)),
-        vmem((CB // 2, 4 * cap)),
-        vmem((CB // 2, 4 * cap)),
         vmem((4, 4 * cap, 2 * CB)),
         *pair((CHUNKS, 2)),
         *pair((CHUNKS, 2)),
@@ -488,12 +465,8 @@
         *pair((3,)),
         *pair((3,)),
         *pair((3,)),
-        *pair((CHUNKS, 2)),
-        *pair((CHUNKS, 2)),
-        *pair((CHUNKS, 2)),
-        *pair((2,)),
-        *pair((2,)),
-        *pair((2,)),
+        *pair((CHUNKS, 3)),
+        *pair((3,)),
     ]
     z, g = pl.pallas_call(
         functools.partial(kernel, n_z, n_cov, cap, float(samples - n_cov)),

time: 110 us -> 96 us (0.87)
  Pallas kernels: 104 us -> 89.9 us
    pallas_call x1, Pallas kernels: 104 us -> 89.9 us  [shards(): pl.pallas_call(functools.partial(kernel, n_z, n_cov, cap, float(samples -...]
where the time goes in v5:
time: 96 us; the launch traced here: 95.8 us
  Pallas kernels  89.9 us (94%)
  other arithmetic  3.76 us (4%)
  local copies, waits for them, and re-layouts  1.45 us (2%)
    pallas_call x1, Pallas kernels, shards(): pl.pallas_call(functools.partial(kernel, n_z, n_cov, cap, float(samples -...  89.9 us
    convert_element_type x1, other arithmetic, shards(): return (z.astype(F32), g / F32(samples))  2.09 us

profile of v5, /device:TPU:1, one launch (start us, length us, event | category | flops | bytes accessed | tf_op | source)
XLA Modules:
  0.0 95.8 jit_solution(1194667981311643786)
XLA Ops:
  0.6 1.5 %copy.8.hcnt = s32[64,4,1]{2,1,0:T(4,128)} copy(s32[64,4,1]{0,1,2:T(4,128)} %bitcast.1) | data formatting | bytes 2048 | tf_op jit(solution)/shard_map/broadcast_in_dim | solution.py:483
  2.1 89.9 %shard_map.68 = (bf16[1024,256]{1,0:T(8,128)(2,1)}, f32[4,128,128]{2,1,0:T(8,128)}) custom-call(bf16[1024,1024]{1,0:T(8,128)(2,1)} %dos.1, bf16[1024,256]{1,0:T(8,128)(2,1)} %prot.1, f32[44,1024]{1,0:T(8,128)} %cov.1, s32[64,4,128]{2,1,0:T(4,128)} %hidx.1, s32[64,4,1]{2,1,0:T(4,128)} %copy.8.hcnt), custom_call_target="tpu_custom_call" | custom-call | tf_op jit(solution)/shard_map/pallas_call | solution.py:471
  92.0 1.7 %broadcast_multiply_fusion = f32[4,128,128]{2,1,0:T(8,128)} fusion(f32[4,128,128]{2,1,0:T(8,128)} %get-tuple-element.5), kind=kLoop, calls=%fused_computation | loop fusion | flops 65536 | bytes 524288 | tf_op jit(solution)/shard_map/div | solution.py:484
  93.7 2.1 %convert_element_type.3 = f32[1024,256]{1,0:T(8,128)} convert(bf16[1024,256]{1,0:T(8,128)(2,1)} %get-tuple-element.4) | non-fusion elementwise | flops 262144 | bytes 1572864 | tf_op jit(solution)/shard_map/convert_element_type | solution.py:484
